TPU v7x, 512 devices: a whole 4x8x8 slice. The times are simulated.
512 devices in a mesh: ctx: 64 (over x, z, core), mp: 8 (over y).
Axes of the slice: x: 4, y: 8, z: 8, core: 2. Of those that a mesh axis runs over, the one named last changes fastest.
Arguments:
- query_proj: bfloat16 [8192, 4096], P(('ctx', 'mp')), may hold values from -91.92388 to 91.92388
- keyval_proj: bfloat16 [8192, 8, 256], P(('ctx', 'mp')), may hold values from -12 to 12
- hidden: bfloat16 [8192, 4096], P('ctx', 'mp'), may hold values from -6 to 6
- weight_x: bfloat16 [4096, 1024], P(None, 'mp'), may hold values from -0.09375 to 0.09375
- conv_x: float32 [4, 1024], P(None, 'mp'), may hold values from -3 to 3
- conv_b: float32 [4, 1024], P(None, 'mp'), may hold values from -3 to 3
- conv_c: float32 [4, 4096], P(None, 'mp'), may hold values from -3 to 3
- step_size: float32 [8192, 32], P('ctx', 'mp'), may hold values from 0 to 1.2, as said below
- decay_log: float32 [32], P('mp'), may hold values from -0.5 to 0.5
- skip_gain: float32 [32], P('mp'), may hold values from 0.5 to 1.5
Outputs:
- student_out: bfloat16 [8192, 4096], P('ctx', 'mp')
- weight_grad: float32 [4096, 1024], P('ctx', 'mp')
Inputs may be any that keep to these rules, and one draw needn't show every extreme that they name: `step_size`: positive.
All inputs are finite; a program needn't handle non-finite values.
Results may differ from a plain program's by a relative error of at most 0.001.
The roundings to bfloat16 on the way count: a program that leaves them out, or rounds other values in their place, can miss the bound.
Values may be sent and summed in bfloat16 or wider, within the bound.
A program may use at most 64 MiB of HBM per device.

v0:
```python
import jax
import jax.numpy as jnp
from jax import lax
from jax.sharding import Mesh
from jax.sharding import PartitionSpec as P

HEAD_TOTAL = 32
KV = 8
HD = 128
CONV = 4
CTX = ("ctx_0", "ctx_1", "ctx_2")
CTX_MP = ("ctx_0", "ctx_1", "ctx_2", "mp")


highest_precision = lax.Precision.HIGHEST
negative = -1e30


def sent_together(arrays, axis, split_dim, concat_dim, along):
    widths = [a.shape[along] for a in arrays]
    both = jnp.concatenate(arrays, axis=along)
    filled = lax.all_to_all(both, axis, split_axis=split_dim, concat_axis=concat_dim, tiled=True)
    return tuple(jnp.split(filled, [sum(widths[:k]) for k in range(1, len(widths))], axis=along))


def laid_out(parts, dim):
    parts = jnp.moveaxis(parts, 0, dim)
    dims = parts.shape
    return parts.reshape(*dims[:dim], dims[dim] * dims[dim + 1], *dims[dim + 2 :])


def all_blocks(array, axes, turns):
    parts = array
    for k in turns:
        parts = lax.all_gather(parts, axes[k])
    done = turns[::-1]
    back = [done.index(k) for k in range(len(axes))]
    parts = parts.transpose(*back, *range(len(axes), parts.ndim))
    return parts.reshape(-1, *array.shape)


def gather_axes(array, axes, turns, dim):
    return laid_out(all_blocks(array, axes, turns), dim)


def sent_to_all(array, axis):
    peers = lax.axis_size(axis)
    return lax.all_to_all(
        jnp.broadcast_to(array[None], (peers, *array.shape)), axis, 0, 0, tiled=True
    )


def gather_directly(array, axis, dim):
    parts = sent_to_all(array, axis)
    return laid_out(parts, dim)


def shifted(value, axis, steps):
    count = lax.axis_size(axis)
    leading, last = (max(0, -steps), min(count, count - steps))
    return lax.ppermute(value, axis, [(source, source + steps) for source in range(leading, last)])


def neutral_like(array, identity):
    return jax.tree.map(
        lambda part, zero: jnp.zeros_like(part) + jnp.asarray(zero, part.dtype), array, identity
    )


def entering(array, axes, combine, identity, reverse):
    before = start = neutral_like(array, identity)
    subtotal = array
    for axis in reversed(axes):
        peers, mine = (lax.axis_size(axis), lax.axis_index(axis))
        pieces = jax.tree.map(lambda part: lax.all_gather(part, axis), subtotal)
        inside, subtotal = (start, start)
        for k in reversed(range(peers)) if reverse else range(peers):
            passed = k > mine if reverse else k < mine
            subtotal = combine(subtotal, jax.tree.map(lambda part: part[k], pieces))
            inside = jax.tree.map(lambda new, old: jnp.where(passed, new, old), subtotal, inside)
        before = combine(inside, before)
    return before


def cut_along(array, dim, peers):
    before, after = (array.shape[:dim], array.shape[dim + 1 :])
    return jnp.moveaxis(array.reshape(*before, peers, -1, *after), dim, 0)


def sum_at_owner(array, axis, dim):
    parts = cut_along(array, dim, lax.axis_size(axis))
    arrived = lax.all_to_all(parts, axis, split_axis=0, concat_axis=0, tiled=True)
    return arrived.sum(axis=0)


def causal_conv(head_rows, signal, kernel):
    length = signal.shape[0]
    extended = jnp.concatenate([head_rows, signal], axis=0).astype(jnp.float32)
    result = jnp.zeros((length, signal.shape[1]), jnp.float32)
    for offset in range(CONV):
        result = result + kernel[offset][None, :] * extended[offset : offset + length]
    return result


def chain_combine(earlier, later):
    return (earlier[0] * later[0], later[0][..., None, None] * earlier[1] + later[1])


def local(
    query_proj,
    keyval_proj,
    hidden,
    weight_x,
    conv_x,
    conv_b,
    conv_c,
    step_size,
    decay_log,
    skip_gain,
):
    groups = KV // lax.axis_size("mp")
    per_group = HEAD_TOTAL // KV
    group_width = per_group * HD
    raw_count = query_proj.shape[0]
    query_grouped = query_proj.reshape(raw_count, KV, group_width)
    query_local, keyval_local = sent_together((query_grouped, keyval_proj), "mp", 1, 0, 2)
    row_count = query_local.shape[0]
    shard_index = lax.axis_index(CTX)
    first_row = shard_index * row_count
    row_positions = first_row + jnp.arange(row_count, dtype=jnp.int32)
    query_total = per_group * row_count
    query_heads = jnp.transpose(
        query_local.reshape(row_count, groups, per_group, HD), (1, 2, 0, 3)
    ).reshape(groups, query_total, HD)
    query_pos = jnp.tile(row_positions, per_group)
    score_scale = HD ** (-0.5)
    start_carry = (
        jnp.full((groups, query_total), negative, jnp.float32),
        jnp.zeros((groups, query_total), jnp.float32),
        jnp.zeros((groups, query_total, HD), jnp.float32),
    )
    shard_piece = gather_axes(keyval_local, CTX, (0, 1, 2), 0)
    piece_rows = shard_piece.shape[0]
    block_size = 512
    block_count = piece_rows // block_size
    blocks = shard_piece.reshape(block_count, block_size, groups, 2 * HD)

    def one_block(inner_carry, block_index):
        row_max, norm_total, weighted = inner_carry
        key_block = lax.dynamic_index_in_dim(blocks, block_index, 0, keepdims=False)
        scores = (
            jnp.einsum(
                "gqd,kgd->gqk",
                query_heads,
                key_block[:, :, :HD],
                preferred_element_type=jnp.float32,
            )
            * score_scale
        )
        key_pos = block_index * block_size + jnp.arange(block_size, dtype=jnp.int32)
        allowed = (key_pos[None, :] <= query_pos[:, None])[None]
        scores = jnp.where(allowed, scores, negative)
        new_max = jnp.maximum(row_max, jnp.max(scores, axis=2))
        weights = jnp.where(allowed, jnp.exp(scores - new_max[:, :, None]), 0.0)
        factor = jnp.exp(row_max - new_max)
        norm_total = norm_total * factor + jnp.sum(weights, axis=2)
        mixed = jnp.einsum(
            "gqk,kgd->gqd",
            weights.astype(jnp.bfloat16),
            key_block[:, :, HD:],
            preferred_element_type=jnp.float32,
        )
        weighted = weighted * factor[:, :, None] + mixed
        return ((new_max, norm_total, weighted), None)

    result, unused = lax.scan(one_block, start_carry, jnp.arange(block_count, dtype=jnp.int32))
    row_max, norm_total, weighted = result
    target = jnp.transpose(
        (weighted / norm_total[..., None]).reshape(groups, per_group, row_count, HD), (2, 0, 1, 3)
    )
    hidden_whole = gather_directly(hidden, "mp", 1)
    x_input = jnp.dot(hidden_whole, weight_x, preferred_element_type=jnp.float32).astype(
        jnp.bfloat16
    )
    rim_width = CONV - 1
    x_width = groups * HD
    key_rows = keyval_local[:, :, :HD].reshape(row_count, x_width)
    query_rows = query_local.reshape(row_count, groups * group_width)
    tail_rows = jnp.concatenate(
        [x_input[-rim_width:], key_rows[-rim_width:], query_rows[-rim_width:]], axis=1
    )
    before = shifted(tail_rows, CTX, 1)
    x_pre = causal_conv(before[:, :x_width], x_input, conv_x)
    x_conv = jax.nn.silu(x_pre)
    b_conv = jax.nn.silu(causal_conv(before[:, x_width : 2 * x_width], key_rows, conv_b))
    c_conv = jax.nn.silu(causal_conv(before[:, 2 * x_width :], query_rows, conv_c))
    x_groups = x_conv.reshape(row_count, groups, HD)
    input_proj_groups = b_conv.reshape(row_count, groups, HD)
    readout_heads = c_conv.reshape(row_count, groups, per_group, HD)
    step_heads = step_size.reshape(row_count, groups, per_group)
    decay_rate = -jnp.exp(decay_log).reshape(groups, per_group)
    skip_heads = skip_gain.reshape(groups, per_group)
    log_decay = jnp.cumsum(step_heads * decay_rate[None], axis=0)
    ordered = jnp.transpose(log_decay, (1, 2, 0))
    causal = jnp.arange(row_count)[:, None] >= jnp.arange(row_count)[None, :]
    differ = ordered[:, :, :, None] - ordered[:, :, None, :]
    within = jnp.where(causal, jnp.exp(jnp.where(causal, differ, 0.0)), 0.0)
    pairwise_scores = jnp.einsum(
        "qmzo,imo->mzqi", readout_heads, input_proj_groups, precision=highest_precision
    )
    mixing_weights = pairwise_scores * within
    driven_state = step_heads[..., None] * x_groups[:, :, None, :]
    inner_portion = jnp.einsum(
        "hewl,lhen->when", mixing_weights, driven_state, precision=highest_precision
    )
    to_end = jnp.exp(log_decay[-1][None] - log_decay)
    local_state = jnp.einsum(
        "sgn,sgrp->grnp",
        input_proj_groups,
        to_end[..., None] * driven_state,
        precision=highest_precision,
    )
    block_decay = jnp.exp(log_decay[-1])
    identity = (jnp.ones_like(block_decay), jnp.zeros_like(local_state))
    chained = entering((block_decay, local_state), CTX, chain_combine, identity, False)
    incoming = chained[1]
    growth = jnp.exp(log_decay)
    carried = growth[..., None] * jnp.einsum(
        "tgrn,grnp->tgrp", readout_heads, incoming, precision=highest_precision
    )
    student = inner_portion + carried + skip_heads[None, :, :, None] * x_groups[:, :, None, :]
    upstream_gradient = 2.0 * (student - target) / (HEAD_TOTAL * HD)
    state_grad = jnp.einsum(
        "tgrn,tgrp->grnp",
        growth[..., None] * readout_heads,
        upstream_gradient,
        precision=highest_precision,
    )
    reverse = entering((block_decay, state_grad), CTX, chain_combine, identity, True)
    later_grad = reverse[1]
    inner_backward = jnp.einsum(
        "lvyq,ylve->qlve", mixing_weights, upstream_gradient, precision=highest_precision
    )
    back_state = to_end[..., None] * jnp.einsum(
        "sgn,grnp->sgrp", input_proj_groups, later_grad, precision=highest_precision
    )
    head_grad = (
        step_heads[..., None] * (inner_backward + back_state)
        + skip_heads[None, :, :, None] * upstream_gradient
    )
    x_grad = jnp.sum(head_grad, axis=2).reshape(row_count, x_width)
    sigmoid_x = jax.nn.sigmoid(x_pre)
    pre_grad = x_grad * sigmoid_x * (1.0 + x_pre * (1.0 - sigmoid_x))
    after = shifted(pre_grad[:rim_width], CTX, -1)
    extended = jnp.concatenate([pre_grad, after], axis=0)
    input_grad = jnp.zeros_like(pre_grad)
    for offset in range(CONV):
        input_grad = (
            input_grad
            + conv_x[offset][None, :] * extended[CONV - 1 - offset : CONV - 1 - offset + row_count]
        )
    input_rounded = input_grad.astype(jnp.bfloat16)
    weight_grad = sum_at_owner(
        lax.dot_general(
            hidden_whole,
            input_rounded,
            (((0,), (0,)), ((), ())),
            preferred_element_type=jnp.float32,
        ),
        CTX,
        0,
    )
    student_out = student.reshape(row_count, groups * group_width).astype(jnp.bfloat16)
    return (student_out, weight_grad)


def solution(mesh):
    finer = Mesh(mesh.devices.reshape(4, 8, 2, mesh.shape["mp"]), ("ctx_0", "ctx_1", "ctx_2", "mp"))
    placed = (
        P(CTX_MP, None),
        P(CTX_MP, None, None),
        P(CTX, "mp"),
        P(None, "mp"),
        P(None, "mp"),
        P(None, "mp"),
        P(None, "mp"),
        P(CTX, "mp"),
        P("mp"),
        P("mp"),
    )
    return jax.shard_map(
        local, mesh=finer, in_specs=placed, out_specs=(P(CTX, "mp"), P(CTX, "mp")), check_vma=False
    )
```

profile of v0, /device:TPU:1, one launch (start us, length us, event | category | flops | bytes accessed | tf_op | source)
XLA Modules:
  0.0 468.6 jit_solution(290495204699570446)
XLA Ops:
  9.8 7.8 %all-to-all-start.1 = ((bf16[16,8,768]{2,0,1:T(8,128)(2,1)}), bf16[16,8,768]{2,0,1:T(8,128)(2,1)S(1)}, u32[]{:S(2)}, u32[]{:S(2)}) async-start(bf16[16,8,768]{2,0,1:T(8,128)(2,1)} %pad_maximum_fusion), calls=%async_computation.1 | async-start | bytes 393216 | tf_op jit(solution)/shard_map/all_to_all | solution.py:22
  19.1 1.0 copy.87
  20.1 6.2 %all-to-all-done.1 = bf16[16,8,768]{2,0,1:T(8,128)(2,1)S(1)} async-done(((bf16[16,8,768]{2,0,1:T(8,128)(2,1)}), bf16[16,8,768]{2,0,1:T(8,128)(2,1)S(1)}, u32[]{:S(2)}, u32[]{:S(2)}) %all-to-all-start.1) | async-done | bytes 196640 | tf_op jit(solution)/shard_map/all_to_all | solution.py:22
  26.3 1.1 broadcast_in_dim.61
  27.4 3.6 all-to-all-start
  31.2 5.0 %all_gather.66 = f32[2,1,4]{2,1,0:T(1,128)S(1)} all-gather(f32[1,1,4]{2,1,0:T(1,128)S(1)} %get-tuple-element.139), channel_id=1, replica_groups=mesh['ctx_0'=4,'ctx_1'=8,'ctx_2'=2,'mp'=8] {'ctx_2'}, dimensions={0}, use_global_device_ids=true | all-gather | bytes 48 | tf_op jit(solution)/shard_map/all_gather | solution.py:75
  38.1 18.9 %all-to-all-done = bf16[8,128,512]{1,2,0:T(8,128)(2,1)S(1)} async-done(((bf16[8,128,512]{1,2,0:T(8,128)(2,1)}), bf16[8,128,512]{1,2,0:T(8,128)(2,1)S(1)}, u32[]{:S(2)}, u32[]{:S(2)}) %all-to-all-start) | async-done | bytes 1048608 | tf_op jit(solution)/shard_map/all_to_all | solution.py:48
  57.5 7.5 %collective-permute-start = (bf16[3,768]{1,0:T(4,128)(2,1)S(1)}, bf16[3,768]{1,0:T(4,128)(2,1)S(1)}, u32[]{:S(2)}, u32[]{:S(2)}) collective-permute-start(bf16[3,768]{1,0:T(4,128)(2,1)S(1)} %pad_maximum_fusion.2), channel_id=1, source_target_pairs={{0,8},{8,16},{16,24},{24,32},{32,40},{40,48},{48,56},{56,64},{64,7... | collective-permute-start | bytes 13832 | tf_op jit(solution)/shard_map/ppermute | solution.py:61
  67.2 2.2 all-gather
  69.4 1.5 bitcast_add_fusion.10
  71.0 15.9 %all-gather.1 = bf16[512,1,256]{2,0,1:T(8,128)(2,1)} all-gather(bf16[128,1,256]{2,0,1:T(8,128)(2,1)S(1)} %split.9), channel_id=3, replica_groups=mesh['ctx_0'=4,'ctx_1'=8,'ctx_2'=2,'mp'=8] {'ctx_0'}, dimensions={0}, use_global_device_ids=true | all-gather | bytes 327680 | tf_op jit(solution)/shard_map/all_gather | solution.py:35
  87.0 14.2 %all_gather.67 = f32[8,1,4]{2,1,0:T(1,128)S(1)} all-gather(f32[1,1,4]{2,1,0:T(1,128)S(1)} %copy-done.42), channel_id=1, replica_groups=mesh['ctx_0'=4,'ctx_1'=8,'ctx_2'=2,'mp'=8] {'ctx_1'}, dimensions={0}, use_global_device_ids=true | all-gather | bytes 144 | tf_op jit(solution)/shard_map/all_gather | solution.py:75
  102.9 9.0 %all-gather.12.cloned.1.call-done = f32[8,1,4,128,128]{4,3,2,1,0:T(8,128)} async-done(((f32[1,1,4,128,128]{4,3,2,1,0:T(8,128)}), f32[8,1,4,128,128]{4,3,2,1,0:T(8,128)}) %all-gather.12.cloned.1.call-update) | async-done | bytes 2097168 | tf_op jit(solution)/shard_map/all_gather | solution.py:75
  111.9 2.4 multiply_add_fusion
  114.4 42.3 %all-gather.20.cloned.1.call-done = bf16[32,128,1,256]{3,1,2,0:T(8,128)(2,1)} async-done(((bf16[4,128,1,256]{3,1,2,0:T(8,128)(2,1)}), bf16[32,128,1,256]{3,1,2,0:T(8,128)(2,1)}) %all-gather.20.cloned.1.call-update) | async-done | bytes 2097168 | tf_op jit(solution)/shard_map/all_gather | solution.py:35
  156.8 7.6 %all_gather.68 = f32[4,1,4]{2,1,0:T(1,128)S(1)} all-gather(f32[1,1,4]{2,1,0:T(1,128)S(1)} %get-tuple-element.148), channel_id=1, replica_groups=mesh['ctx_0'=4,'ctx_1'=8,'ctx_2'=2,'mp'=8] {'ctx_0'}, dimensions={0}, use_global_device_ids=true | all-gather | bytes 80 | tf_op jit(solution)/shard_map/all_gather | solution.py:75
  166.5 22.8 %all-gather.14.cloned.1.call-done = f32[4,1,4,128,128]{4,3,2,1,0:T(8,128)} async-done(((f32[1,1,4,128,128]{4,3,2,1,0:T(8,128)}), f32[4,1,4,128,128]{4,3,2,1,0:T(8,128)}) %all-gather.14.cloned.1.call-update) | async-done | bytes 1048592 | tf_op jit(solution)/shard_map/all_gather | solution.py:75
  189.4 2.8 fusion.19
  192.3 1.1 fusion.217
  193.4 22.5 %all-gather.22.cloned.1.call-done = bf16[16,4,128,1,256]{4,2,3,1,0:T(8,128)(2,1)} async-done(((bf16[8,4,128,1,256]{4,2,3,1,0:T(8,128)(2,1)}), bf16[16,4,128,1,256]{4,2,3,1,0:T(8,128)(2,1)}) %all-gather.22.cloned.1.call-update) | async-done | bytes 4194320 | tf_op jit(solution)/shard_map/all_gather | solution.py:35
  215.9 4.7 %copy.103 = bf16[4,8,2,128,1,256]{5,3,2,1,0,4:T(8,128)(2,1)} copy(bf16[4,8,2,128,1,256]{5,3,0,1,2,4:T(8,128)(2,1)} %bitcast.410) | data formatting | bytes 8388608 | tf_op jit(solution)/shard_map/transpose | solution.py:38
  220.7 84.9 %while.15 = (s32[]{:T(128)}, f32[1,512]{1,0:T(1,128)S(1)}, f32[1,512]{1,0:T(1,128)S(1)}, f32[1,512,128]{2,1,0:T(8,128)S(1)}, s32[16]{0:T(128)S(1)}, /*index=5*/b...) while((s32[]{:T(128)}, f32[1,512]{1,0:T(1,128)S(1)}, ...), condition=%wide.region_4.5_spmd.clone, body=%wide.region_1.0_spmd.clone.sunk | while | flops 137563136 | bytes 4637387 | solution.py:176
  223.9 1.0 dynamic-slice_bitcast_fusion.2
  229.2 1.0 dynamic-slice_bitcast_fusion.2
  234.5 1.0 dynamic-slice_bitcast_fusion.2
  239.8 1.0 dynamic-slice_bitcast_fusion.2
  245.1 1.0 dynamic-slice_bitcast_fusion.2
  250.4 1.0 dynamic-slice_bitcast_fusion.2
  255.7 1.0 dynamic-slice_bitcast_fusion.2
  261.0 1.0 dynamic-slice_bitcast_fusion.2
  266.3 1.0 dynamic-slice_bitcast_fusion.2
  271.6 1.0 dynamic-slice_bitcast_fusion.2
  287.6 1.0 dynamic-slice_bitcast_fusion.2
  292.9 1.0 dynamic-slice_bitcast_fusion.2
  298.2 1.0 dynamic-slice_bitcast_fusion.2
  306.6 2.2 all-gather.4
  310.5 40.5 %all-gather.16.cloned.1.call-done = f32[8,1,4,128,128]{4,3,2,1,0:T(8,128)} async-done(((f32[1,1,4,128,128]{4,3,2,1,0:T(8,128)}), f32[8,1,4,128,128]{4,3,2,1,0:T(8,128)}) %all-gather.16.cloned.1.call-update) | async-done | bytes 2097168 | tf_op jit(solution)/shard_map/all_gather | solution.py:75
  351.1 2.5 slice_add_fusion.4
  353.6 7.6 %all_gather.79 = f32[4,1,4]{2,1,0:T(1,128)S(1)} all-gather(f32[1,1,4]{2,1,0:T(1,128)S(1)} %copy-done.45), channel_id=1, replica_groups=mesh['ctx_0'=4,'ctx_1'=8,'ctx_2'=2,'mp'=8] {'ctx_0'}, dimensions={0}, use_global_device_ids=true | all-gather | bytes 80 | tf_op jit(solution)/shard_map/all_gather | solution.py:75
  362.9 21.4 %all-gather.18.cloned.1.call-done = f32[4,1,4,128,128]{4,3,2,1,0:T(8,128)} async-done(((f32[1,1,4,128,128]{4,3,2,1,0:T(8,128)}), f32[4,1,4,128,128]{4,3,2,1,0:T(8,128)}) %all-gather.18.cloned.1.call-update) | async-done | bytes 1048592 | tf_op jit(solution)/shard_map/all_gather | solution.py:75
  384.3 2.8 fusion.25
  387.9 3.5 collective-permute-start.1
  391.4 2.5 collective-permute-done.1
  393.9 2.4 convolution_bitcast_fusion.1
  396.3 2.9 copy.112
  399.3 9.0 %all-to-all-start.2 = ((f32[64,64,128]{2,1,0:T(8,128)}), f32[64,64,128]{2,1,0:T(8,128)}, u32[]{:S(2)}, u32[]{:S(2)}) async-start(f32[64,64,128]{2,1,0:T(8,128)} %bitcast.408), calls=%async_computation.2 | async-start | bytes 4194304 | tf_op jit(solution)/shard_map/all_to_all | solution.py:92
  409.0 50.4 %all-to-all-done.2 = f32[64,64,128]{2,1,0:T(8,128)} async-done(((f32[64,64,128]{2,1,0:T(8,128)}), f32[64,64,128]{2,1,0:T(8,128)}, u32[]{:S(2)}, u32[]{:S(2)}) %all-to-all-start.2) | async-done | bytes 2097184 | tf_op jit(solution)/shard_map/all_to_all | solution.py:92
  459.4 2.3 reduce_sum.30
  (321 shorter events, 48.6 us)
Async XLA Ops:
  7.2 49.9 %copy-start = (bf16[4096,128]{1,0:T(8,128)(2,1)S(1)}, bf16[4096,128]{1,0:T(8,128)(2,1)}, u32[]{:S(2)}) copy-start(bf16[4096,128]{1,0:T(8,128)(2,1)} %param.15) | copy-start | bytes 3145732
  9.8 27.7 %copy-start.43 = (f32[4,128]{1,0:T(4,128)S(1)}, f32[4,128]{1,0:T(4,128)}, u32[]{:S(2)}) copy-start(f32[4,128]{1,0:T(4,128)} %param.16) | copy-start | bytes 6148
  9.8 27.7 %copy-start.44 = (f32[4,128]{1,0:T(4,128)S(1)}, f32[4,128]{1,0:T(4,128)}, u32[]{:S(2)}) copy-start(f32[4,128]{1,0:T(4,128)} %param.17) | copy-start | bytes 6148
  9.8 16.5 %all-to-all-start.1 = ((bf16[16,8,768]{2,0,1:T(8,128)(2,1)}), bf16[16,8,768]{2,0,1:T(8,128)(2,1)S(1)}, u32[]{:S(2)}, u32[]{:S(2)}) async-start(bf16[16,8,768]{2,0,1:T(8,128)(2,1)} %pad_maximum_fusion), calls=%async_computation.1 | async-start | bytes 393216 | tf_op jit(solution)/shard_map/all_to_all | solution.py:22
  27.4 29.6 %all-to-all-start = ((bf16[8,128,512]{1,2,0:T(8,128)(2,1)}), bf16[8,128,512]{1,2,0:T(8,128)(2,1)S(1)}, u32[]{:S(2)}, u32[]{:S(2)}) async-start(bf16[8,128,512]{1,2,0:T(8,128)(2,1)} %broadcast_in_dim.61), calls=%async_computation | async-start | bytes 2097152 | tf_op jit(solution)/shard_map/all_to_all | solution.py:48
  31.0 35.8 %copy-start.7 = (f32[128,4]{0,1:T(4,128)S(1)}, f32[128,4]{0,1:T(4,128)}, u32[]{:S(2)}) copy-start(f32[128,4]{0,1:T(4,128)} %param.19) | copy-start | bytes 6148
  31.0 80.9 %all-gather.12.cloned.1.call-start = ((), (), s32[]{:S(2)}) async-start(), calls=%async_computation.3 | async-start | bytes 2359296 | tf_op jit(solution)/shard_map/all_gather | solution.py:75
  37.5 29.2 %copy-start.26 = (f32[128]{0:T(128)}, f32[128]{0:T(128)S(1)}, u32[]{:S(2)}) copy-start(f32[128]{0:T(128)S(1)} %get-tuple-element.173) | copy-start | bytes 1540
  37.5 29.2 %copy-start.28 = (f32[128]{0:T(128)}, f32[128]{0:T(128)S(1)}, u32[]{:S(2)}) copy-start(f32[128]{0:T(128)S(1)} %get-tuple-element.174) | copy-start | bytes 1540
  37.5 29.2 %copy-start.30 = (f32[128]{0:T(128)}, f32[128]{0:T(128)S(1)}, u32[]{:S(2)}) copy-start(f32[128]{0:T(128)S(1)} %get-tuple-element.175) | copy-start | bytes 1540
  37.5 29.2 %copy-start.31 = (f32[128]{0:T(128)}, f32[128]{0:T(128)S(1)}, u32[]{:S(2)}) copy-start(f32[128]{0:T(128)S(1)} %get-tuple-element.176) | copy-start | bytes 1540
  38.1 29.1 %copy-start.13 = (f32[128,4]{0,1:T(4,128)}, f32[128,4]{0,1:T(4,128)S(1)}, u32[]{:S(2)}) copy-start(f32[128,4]{0,1:T(4,128)S(1)} %get-tuple-element.164) | copy-start | bytes 6148
  57.5 8.3 %collective-permute-start = (bf16[3,768]{1,0:T(4,128)(2,1)S(1)}, bf16[3,768]{1,0:T(4,128)(2,1)S(1)}, u32[]{:S(2)}, u32[]{:S(2)}) collective-permute-start(bf16[3,768]{1,0:T(4,128)(2,1)S(1)} %pad_maximum_fusion.2), channel_id=1, source_target_pairs={{0,8},{8,16},{16,24},{24,32},{32,40},{40,48},{48,56},{56,64},{64,7... | collective-permute-start | bytes 13832 | tf_op jit(solution)/shard_map/ppermute | solution.py:61
  66.5 20.5 %copy-start.42 = (f32[1,1,4]{2,1,0:T(1,128)S(1)}, f32[1,1,4]{2,1,0:T(1,128)}, u32[]{:S(2)}) copy-start(f32[1,1,4]{2,1,0:T(1,128)} %get-tuple-element.179) | copy-start | bytes 52
  70.9 85.8 %all-gather.20.cloned.1.call-start = ((), (), s32[]{:S(2)}) async-start(), calls=%async_computation.7 | async-start | bytes 2359296 | tf_op jit(solution)/shard_map/all_gather | solution.py:35
  86.9 102.4 %all-gather.14.cloned.1.call-start = ((), (), s32[]{:S(2)}) async-start(), calls=%async_computation.4 | async-start | bytes 1310720 | tf_op jit(solution)/shard_map/all_gather | solution.py:75
  102.3 87.0 %copy-start.32 = (f32[4]{0:T(128)}, f32[4]{0:T(128)S(1)}, u32[]{:S(2)}) copy-start(f32[4]{0:T(128)S(1)} %get-tuple-element.150) | copy-start | bytes 52
  102.3 87.0 %copy-start.34 = (f32[4]{0:T(128)}, f32[4]{0:T(128)S(1)}, u32[]{:S(2)}) copy-start(f32[4]{0:T(128)S(1)} %get-tuple-element.151) | copy-start | bytes 52
  102.9 86.5 %copy-start.18 = (f32[4]{0:T(128)}, f32[4]{0:T(128)S(1)}, u32[]{:S(2)}) copy-start(f32[4]{0:T(128)S(1)} %get-tuple-element.156) | copy-start | bytes 52
  102.9 86.5 %copy-start.20 = (f32[4]{0:T(128)}, f32[4]{0:T(128)S(1)}, u32[]{:S(2)}) copy-start(f32[4]{0:T(128)S(1)} %get-tuple-element.157) | copy-start | bytes 52
  102.9 86.5 %copy-start.22 = (f32[4]{0:T(128)}, f32[4]{0:T(128)S(1)}, u32[]{:S(2)}) copy-start(f32[4]{0:T(128)S(1)} %get-tuple-element.158) | copy-start | bytes 52
  102.9 86.5 %copy-start.24 = (f32[4]{0:T(128)}, f32[4]{0:T(128)S(1)}, u32[]{:S(2)}) copy-start(f32[4]{0:T(128)S(1)} %get-tuple-element.155) | copy-start | bytes 52
  111.9 53.1 %copy-start.10 = (f32[2,1,4]{2,1,0:T(1,128)S(1)}, f32[2,1,4]{2,1,0:T(1,128)}, u32[]{:S(2)}) copy-start(f32[2,1,4]{2,1,0:T(1,128)} %copy-done.9) | copy-start | bytes 100
  111.9 53.2 %copy-start.17 = (f32[4,512]{1,0:T(4,128)S(1)}, f32[4,512]{1,0:T(4,128)}, u32[]{:S(2)}) copy-start(f32[4,512]{1,0:T(4,128)} %param.18) | copy-start | bytes 24580
  114.3 51.5 %slice-start = ((bf16[3,768]{1,0:T(4,128)(2,1)}), bf16[3,512]{1,0:T(4,128)(2,1)S(1)}, s32[]{:S(2)}) async-start(bf16[3,768]{1,0:T(4,128)(2,1)} %copy-done.8), calls=%async_computation.9 | async-start | bytes 8192 | tf_op jit(solution)/shard_map/slice | solution.py:196
  114.4 101.5 %all-gather.22.cloned.1.call-start = ((), (), s32[]{:S(2)}) async-start(), calls=%async_computation.8 | async-start | bytes 6291456 | tf_op jit(solution)/shard_map/all_gather | solution.py:35
  156.7 32.7 %copy-start.15 = (f32[128,4]{0,1:T(4,128)S(1)}, f32[128,4]{0,1:T(4,128)}, u32[]{:S(2)}) copy-start(f32[128,4]{0,1:T(4,128)} %get-tuple-element.163) | copy-start | bytes 6148
  156.7 32.7 %copy-start.38 = (f32[4]{0:T(128)S(1)}, f32[4]{0:T(128)}, u32[]{:S(2)}) copy-start(f32[4]{0:T(128)} %get-tuple-element.178) | copy-start | bytes 52
  156.8 32.7 %copy-start.41 = (f32[4]{0:T(128)S(1)}, f32[4]{0:T(128)}, u32[]{:S(2)}) copy-start(f32[4]{0:T(128)} %get-tuple-element.181) | copy-start | bytes 52
  156.8 194.3 %all-gather.16.cloned.1.call-start = ((), (), s32[]{:S(2)}) async-start(), calls=%async_computation.5 | async-start | bytes 2359296 | tf_op jit(solution)/shard_map/all_gather | solution.py:75
  220.7 85.3 %copy-start.16 = (f32[128,4]{0,1:T(4,128)S(1)}, f32[128,4]{0,1:T(4,128)}, u32[]{:S(2)}) copy-start(f32[128,4]{0,1:T(4,128)} %get-tuple-element.163) | copy-start | bytes 6148
  305.6 45.4 %copy-start.19 = (f32[4]{0:T(128)S(1)}, f32[4]{0:T(128)}, u32[]{:S(2)}) copy-start(f32[4]{0:T(128)} %copy-done.18) | copy-start | bytes 52
  305.6 45.4 %copy-start.21 = (f32[4]{0:T(128)S(1)}, f32[4]{0:T(128)}, u32[]{:S(2)}) copy-start(f32[4]{0:T(128)} %copy-done.20) | copy-start | bytes 52
  305.6 45.4 %copy-start.23 = (f32[4]{0:T(128)S(1)}, f32[4]{0:T(128)}, u32[]{:S(2)}) copy-start(f32[4]{0:T(128)} %copy-done.22) | copy-start | bytes 52
  305.7 45.4 %copy-start.25 = (f32[4]{0:T(128)S(1)}, f32[4]{0:T(128)}, u32[]{:S(2)}) copy-start(f32[4]{0:T(128)} %copy-done.24) | copy-start | bytes 52
  305.7 45.4 %copy-start.33 = (f32[4]{0:T(128)S(1)}, f32[4]{0:T(128)}, u32[]{:S(2)}) copy-start(f32[4]{0:T(128)} %copy-done.32) | copy-start | bytes 52
  305.7 45.4 %copy-start.35 = (f32[4]{0:T(128)S(1)}, f32[4]{0:T(128)}, u32[]{:S(2)}) copy-start(f32[4]{0:T(128)} %copy-done.34) | copy-start | bytes 52
  305.7 45.4 %copy-start.37 = (f32[4]{0:T(128)S(1)}, f32[4]{0:T(128)}, u32[]{:S(2)}) copy-start(f32[4]{0:T(128)} %get-tuple-element.154) | copy-start | bytes 52
  305.7 45.4 %copy-start.40 = (f32[4]{0:T(128)S(1)}, f32[4]{0:T(128)}, u32[]{:S(2)}) copy-start(f32[4]{0:T(128)} %get-tuple-element.152) | copy-start | bytes 52
  308.8 44.7 %copy-start.45 = (f32[1,1,4]{2,1,0:T(1,128)S(1)}, f32[1,1,4]{2,1,0:T(1,128)}, u32[]{:S(2)}) copy-start(f32[1,1,4]{2,1,0:T(1,128)} %get-tuple-element.147) | copy-start | bytes 52
  308.8 52.3 %copy-start.47 = (f32[4]{0:T(128)S(1)}, f32[4]{0:T(128)}, u32[]{:S(2)}) copy-start(f32[4]{0:T(128)} %param.21) | copy-start | bytes 52
  308.8 52.9 %copy-start.11 = (f32[2,1,4]{2,1,0:T(1,128)S(1)}, f32[2,1,4]{2,1,0:T(1,128)}, u32[]{:S(2)}) copy-start(f32[2,1,4]{2,1,0:T(1,128)} %copy-done.9) | copy-start | bytes 100
  308.8 75.4 %copy-start.14 = (f32[128,4]{0,1:T(4,128)S(1)}, f32[128,4]{0,1:T(4,128)}, u32[]{:S(2)}) copy-start(f32[128,4]{0,1:T(4,128)} %copy-done.13) | copy-start | bytes 6148
  310.4 73.8 %copy-start.2 = (f32[1,1,4,128,128]{4,3,2,1,0:T(8,128)S(1)}, f32[1,1,4,128,128]{4,3,2,1,0:T(8,128)}, u32[]{:S(2)}) copy-start(f32[1,1,4,128,128]{4,3,2,1,0:T(8,128)} %fusion.33) | copy-start | bytes 786436
  310.4 73.8 %all-gather.18.cloned.1.call-start = ((), (), s32[]{:S(2)}) async-start(), calls=%async_computation.6 | async-start | bytes 1310720 | tf_op jit(solution)/shard_map/all_gather | solution.py:75
  384.3 9.7 %copy-start.27 = (f32[128]{0:T(128)S(1)}, f32[128]{0:T(128)}, u32[]{:S(2)}) copy-start(f32[128]{0:T(128)} %copy-done.26) | copy-start | bytes 1540
  387.9 6.0 %collective-permute-start.1 = (f32[3,128]{1,0:T(4,128)S(1)}, f32[3,128]{1,0:T(4,128)S(1)}, u32[]{:S(2)}, u32[]{:S(2)}) collective-permute-start(f32[3,128]{1,0:T(4,128)S(1)} %slice.434), channel_id=1, source_target_pairs={{8,0},{16,8},{24,16},{32,24},{40,32},{48,40},{56,48},{64,56},{72,6... | collective-permute-start | bytes 4616 | tf_op jit(solution)/shard_map/ppermute | solution.py:61
  399.3 60.1 %all-to-all-start.2 = ((f32[64,64,128]{2,1,0:T(8,128)}), f32[64,64,128]{2,1,0:T(8,128)}, u32[]{:S(2)}, u32[]{:S(2)}) async-start(f32[64,64,128]{2,1,0:T(8,128)} %bitcast.408), calls=%async_computation.2 | async-start | bytes 4194304 | tf_op jit(solution)/shard_map/all_to_all | solution.py:92
  (13 other events, 53.9 us)
Sparse Core Ops, SparseCore 0:
  71.0 40.8 all-gather.11
  114.0 42.7 all-gather.19
  158.8 30.5 all-gather.13
  191.3 24.5 all-gather.21
  310.6 40.4 all-gather.15
  353.7 30.5 all-gather.17
where the time goes:
time: 470 us; the launch traced here: 469 us
  waiting for transfers between devices  237 us (50%)
  blocking collectives  54.7 us (12%)
  loops' own time  42.5 us (9%)
  local copies, waits for them, and re-layouts  40.6 us (9%)
  starting transfers between devices  31.5 us (7%)
  matrix products  24.7 us (5%)
  other arithmetic  22.5 us (5%)
  between operations  14.8 us (3%)
    all_gather x4, waiting for transfers between devices, entering(): pieces = jax.tree.map(lambda part: lax.all_gather(part, axis), subtotal)  93.7 us
    all_gather x2, waiting for transfers between devices, all_blocks(): parts = lax.all_gather(parts, axes[k])  64.8 us
    all_to_all x1, waiting for transfers between devices, sum_at_owner(): lax.all_to_all(parts, axis, split_axis=0, concat_axis=0, tiled=True)  50.4 us
    another operation x1, loops' own time, local(): lax.scan(one_block, start_carry, jnp.arange(block_count, dtype=jnp.int32))  42.5 us
    all_gather x6, blocking collectives, entering(): pieces = jax.tree.map(lambda part: lax.all_gather(part, axis), subtotal)  38.7 us
    all_to_all x1, waiting for transfers between devices, sent_to_all(): lax.all_to_all(jnp.broadcast_to(array[None], (peers, *array.shape)), axis...  18.9 us
    all_gather x1, blocking collectives, all_blocks(): parts = lax.all_gather(parts, axes[k])  15.9 us
    squeeze x16, local copies, waits for them, and re-layouts, one_block(): key_block = lax.dynamic_index_in_dim(blocks, block_index, 0, keepdims=False)  15.6 us
  transfers between devices with their start and end apart: 11, of which 11 were waited for; matrix products, arithmetic and copies ran while one was open for 4% of the time, Pallas kernels for 0%

commit v1 on v0

v1 whole, which is shorter than its diff:
```python
import functools

import jax
import jax.numpy as jnp
from jax import lax
from jax.experimental import pallas as pl
from jax.experimental.pallas import tpu as pltpu
from jax.sharding import Mesh
from jax.sharding import PartitionSpec as P

HEAD_TOTAL = 32
KV = 8
HD = 128
CONV = 4
TOK = 128
PER = HEAD_TOTAL // KV
NX, NZ, NK, NM = 4, 8, 2, 8
CTX = ("ctx_0", "ctx_1", "ctx_2")
CTX_MP = ("ctx_0", "ctx_1", "ctx_2", "mp")
MESH = pl.DeviceIdType.MESH
F32, BF16 = jnp.float32, jnp.bfloat16
NEG = -1e30
SCALE2 = HD**-0.5 * 1.4426950408889634


def place():
    return tuple(lax.axis_index(name) for name in CTX_MP)


def remote(src, dst, send, recv, device):
    return pltpu.make_async_remote_copy(
        src_ref=src, dst_ref=dst, send_sem=send, recv_sem=recv, device_id=device, device_id_type=MESH
    )


def greet(devices):
    barrier = pltpu.get_barrier_semaphore()
    for device in devices:
        pl.semaphore_signal(barrier, inc=1, device_id=device, device_id_type=MESH)
    pl.semaphore_wait(barrier, len(devices))


def exact(a, b, dims=((1,), (0,))):
    return lax.dot_general(
        a, b, (dims, ((), ())), precision=lax.Precision.HIGHEST, preferred_element_type=F32
    )


def front(
    q_in, kv_in, hid_in, wx,
    target, q_loc, k_loc, xin, hidq,
    q2, kvb, hall, qs, m_s, l_s, acc, stat, acc_in, stat_in,
    own_sem, yq, ykv, yh, xkv, ring, cq, co, hq,
):
    x, z, k, m = place()
    zr, zl = lax.rem(z + 1, NZ), lax.rem(z + NZ - 1, NZ)
    sibling = (x, z, 1 - k, m)
    y_peers = [(x, z, k, lax.rem(m + d, NM)) for d in range(1, NM)]
    x_peers = [(lax.rem(x + d, NX), z, k, m) for d in range(1, NX)]
    greet([*y_peers, *x_peers, (x, zr, k, m), (x, zl, k, m), sibling])

    rows = pl.ds(pl.multiple_of(m * 16, 16), 16)
    sent = []
    for d in range(1, NM):
        peer = y_peers[d - 1]
        cols = pl.ds(pl.multiple_of(peer[3] * 256, 256), 256)
        sent.append(remote(kv_in.at[:, cols], kvb.at[z, x, rows], ykv.at[0, d - 1], ykv.at[1, d - 1], peer))
        sent[-1].start()
    for d in range(1, NM):
        peer = y_peers[d - 1]
        cols = pl.ds(pl.multiple_of(peer[3] * 512, 512), 512)
        sent.append(remote(q_in.at[:, cols], q2.at[0, rows], yq.at[0, d - 1], yq.at[1, d - 1], peer))
        sent[-1].start()
    y_moves = list(sent)
    for d in range(1, NM):
        sent.append(remote(hid_in, hall.at[m], yh.at[0, d - 1], yh.at[1, d - 1], y_peers[d - 1]))
        sent[-1].start()
    h_moves = sent[len(y_moves) :]
    mine = [
        pltpu.make_async_copy(
            kv_in.at[:, pl.ds(pl.multiple_of(m * 256, 256), 256)], kvb.at[z, x, rows], own_sem.at[0]
        ),
        pltpu.make_async_copy(
            q_in.at[:, pl.ds(pl.multiple_of(m * 512, 512), 512)], q2.at[0, rows], own_sem.at[1]
        ),
        pltpu.make_async_copy(hid_in, hall.at[m], own_sem.at[2]),
    ]
    for move in mine:
        move.start()

    for xs in range(1, NX):

        @pl.when(xs > x)
        def _(xs=xs):
            kvb[:, xs] = jnp.zeros((NZ, TOK, 2 * HD), BF16)

    m_s[...] = jnp.full(m_s.shape, NEG, F32)
    l_s[...] = jnp.zeros(l_s.shape, F32)
    acc[...] = jnp.zeros(acc.shape, F32)
    for move in mine:
        move.wait()

    def ring_copy(way, step, xs):
        if way == 0:
            column, device = lax.rem(z - (step - 1) + NZ, NZ), (x, zr, k, m)
        else:
            column, device = lax.rem(z + (step - 1), NZ), (x, zl, k, m)
        slot = kvb.at[column, xs]
        at = (way * 4 + step - 1) * NX + xs
        return remote(slot, slot, ring.at[0, at], ring.at[1, at], device)

    def x_copy(d):
        slot = kvb.at[z, x]
        return remote(slot, slot, xkv.at[0, d - 1], xkv.at[1, d - 1], (lax.rem(x + d, NX), z, k, m))

    for move in y_moves[: NM - 1]:
        move.wait_recv()
    for d in range(1, NX):

        @pl.when(x + d < NX)
        def _(d=d):
            x_copy(d).start()

    for xs in range(NX):

        @pl.when(xs == x)
        def _(xs=xs):
            ring_copy(0, 1, xs).start()
            ring_copy(1, 1, xs).start()

    for move in y_moves[NM - 1 :]:
        move.wait_recv()
    q_move = remote(q2.at[0], q2.at[1], cq.at[0], cq.at[1], sibling)
    q_move.start()

    for xs in range(NX):
        for d in range(1, NX):
            if xs + d < NX:

                @pl.when(x == xs + d)
                def _(xs=xs, d=d):
                    slot = kvb.at[z, xs]
                    remote(slot, slot, xkv.at[0, d - 1], xkv.at[1, d - 1], sibling).wait_recv()
                    ring_copy(0, 1, xs).start()
                    ring_copy(1, 1, xs).start()

    for h in range(PER):
        qs[0, h * TOK : (h + 1) * TOK] = q2[0, :, h * HD : (h + 1) * HD]
    q_move.wait_recv()
    for h in range(PER):
        qs[1, h * TOK : (h + 1) * TOK] = q2[1, :, h * HD : (h + 1) * HD]

    def attend(column, masked):
        def tile(i, carry):
            side, first = lax.div(i, 2), pl.multiple_of(lax.rem(i, 2) * 256, 256)
            at = pl.ds(first, 256)
            block = kvb[column].reshape(NX * TOK, 2 * HD)
            s = lax.dot_general(
                qs[side, at], block[:, :HD], (((1,), (1,)), ((), ())), preferred_element_type=F32
            )
            if masked:
                key = lax.broadcasted_iota(jnp.int32, (256, NX * TOK), 1)
                row = lax.broadcasted_iota(jnp.int32, (256, NX * TOK), 0)
                core = jnp.where(side == 0, k, 1 - k)
                ahead = (key - x * TOK) + k * TOK - (lax.rem(row, TOK) + core * TOK)
                allowed = (key < x * TOK) | ((ahead <= 0) & (key < (x + 1) * TOK))
                s = jnp.where(allowed, s * SCALE2, NEG)
            else:
                key = lax.broadcasted_iota(jnp.int32, (1, NX * TOK), 1)
                limit = jnp.where(column < z, (x + 1) * TOK, x * TOK)
                s = s * SCALE2 + jnp.where(key < limit, 0.0, NEG)
            before = m_s[side, at, :1]
            now = jnp.maximum(before, jnp.max(s, axis=1, keepdims=True))
            p = jnp.exp2(s - now)
            alpha = jnp.exp2(before - now)
            m_s[side, at] = jnp.broadcast_to(now, (256, HD))
            l_s[side, at] = l_s[side, at] * alpha + jnp.sum(p, axis=1, keepdims=True)
            acc[side, at] = acc[side, at] * alpha + jnp.dot(
                p.astype(BF16), block[:, HD:], preferred_element_type=F32
            )
            return carry

        lax.fori_loop(0, 4, tile, 0)

    attend(z, True)
    for step in range(1, 5):
        for way in range(2):
            for xs in range(NX):
                if way == 0 or step < 4:

                    @pl.when(xs <= x)
                    def _(way=way, xs=xs, step=step):
                        ring_copy(way, step, xs).wait_recv()
                        if step < (4, 3)[way]:
                            ring_copy(way, step + 1, xs).start()

        attend(lax.rem(z - step + NZ, NZ), False)
        if step < 4:
            attend(lax.rem(z + step, NZ), False)

    lane = lax.broadcasted_iota(jnp.int32, (PER * TOK, HD), 1)
    stat[...] = jnp.where(lane < 64, m_s[1], l_s[1])
    o_moves = [
        remote(acc.at[1], acc_in, co.at[0, 0], co.at[1, 0], sibling),
        remote(stat, stat_in, co.at[0, 1], co.at[1, 1], sibling),
    ]
    for move in o_moves:
        move.start()

    for move in h_moves:
        move.wait_recv()
    hq_moves = []
    for d in range(1, NX):
        there = lax.rem(x + d, NX)
        for e in range(2):
            at = (d - 1) * 2 + e
            into = hidq.at[e, pl.ds(pl.multiple_of(x * TOK, TOK), TOK)]
            hq_moves.append(
                remote(hall.at[2 * there + e], into, hq.at[0, at], hq.at[1, at], x_peers[d - 1])
            )
            hq_moves[-1].start()
    for e in range(2):
        hidq[e, pl.ds(pl.multiple_of(x * TOK, TOK), TOK)] = hall[2 * x + e]
    total = jnp.zeros((TOK, HD), F32)
    for j in range(NM):
        total = total + jnp.dot(hall[j], wx[j * 512 : (j + 1) * 512], preferred_element_type=F32)
    xin[...] = total.astype(BF16)
    q_loc[...] = q2[0]
    k_loc[...] = kvb[z, x, :, :HD]

    for move in o_moves:
        move.wait_recv()
    other = stat_in[:, :1]
    mine_max = m_s[0, :, :1]
    both = jnp.maximum(other, mine_max)
    a0, a1 = jnp.exp2(mine_max - both), jnp.exp2(other - both)
    norm = l_s[0, :, :1] * a0 + stat_in[:, 64:65] * a1
    result = (acc[0] * a0 + acc_in[...] * a1) / norm
    for h in range(PER):
        target[:, h * HD : (h + 1) * HD] = result[h * TOK : (h + 1) * TOK]

    for move in hq_moves:
        move.wait_recv()
    for move in [*sent, q_move, *o_moves, *hq_moves]:
        move.wait_send()
    for d in range(1, NX):

        @pl.when(x + d < NX)
        def _(d=d):
            x_copy(d).wait_send()

    for way in range(2):
        for step in range(1, (4, 3)[way] + 1):
            for xs in range(NX):

                @pl.when(xs <= x)
                def _(way=way, step=step, xs=xs):
                    ring_copy(way, step, xs).wait_send()


def silu(v):
    return v / (1.0 + jnp.exp(-v))


def back(
    xin, k_loc, q_loc, target, step_size, decay_log, skip_gain, conv_x, conv_b, conv_c, hidq,
    out_s, out_w,
    ext, ext2, mix, local_state, sgrad, csib, dec, dsib, zsend, zrecv, xsend, xrecv,
    zbs, zbr, cback, inc, ig, part, wrecv, wsend, wzr, up,
    halo, cs, zs, xs_, bs, ks, igs, wc, wz,
):
    x, z, k, m = place()
    c = (x * NZ + z) * NK + k
    last = NX * NZ * NK - 1
    sibling = (x, z, 1 - k, m)

    def at_ctx(i):
        return (lax.div(i, NZ * NK), lax.rem(lax.div(i, NK), NZ), lax.rem(i, NK), m)

    following, previous = at_ctx(lax.rem(c + 1, last + 1)), at_ctx(lax.rem(c + last, last + 1))
    z_peers = [(x, lax.rem(z + d, NZ), k, m) for d in range(1, NZ)]
    x_peers = [(lax.rem(x + d, NX), z, k, m) for d in range(1, NX)]
    greet([*z_peers, *x_peers, sibling, following, previous])
    sent = []

    def go(*args):
        move = remote(*args)
        move.start()
        sent.append(move)
        return move

    ext[8:, :HD] = xin[...].astype(F32)
    ext[8:, HD : 2 * HD] = k_loc[...].astype(F32)
    ext[8:, 2 * HD :] = q_loc[...].astype(F32)
    tail = remote(ext.at[pl.ds(TOK, 8)], ext.at[pl.ds(0, 8)], halo.at[0], halo.at[1], following)

    @pl.when(c < last)
    def _():
        tail.start()

    @pl.when(c == 0)
    def _():
        ext[:8] = jnp.zeros((8, 6 * HD), F32)

    row = lax.broadcasted_iota(jnp.int32, (TOK, TOK), 0)
    col = lax.broadcasted_iota(jnp.int32, (TOK, TOK), 1)
    causal = row >= col
    lower = jnp.where(causal, 1.0, 0.0)
    rate = -jnp.exp(decay_log[...])
    steps, growth, to_end, within = [], [], [], []
    for h in range(PER):
        step = jnp.broadcast_to(step_size[:, h : h + 1], (TOK, TOK))
        log_decay = exact(lower, step * rate[:, h : h + 1])
        final = log_decay[TOK - 1 :]
        steps.append(step)
        growth.append(jnp.exp(log_decay))
        to_end.append(jnp.exp(final - log_decay))
        within.append(
            jnp.where(causal, jnp.exp(jnp.where(causal, log_decay - log_decay.T, 0.0)), 0.0)
        )
        dec[h : h + 1] = jnp.exp(final)
        dec[PER + h : PER + h + 1] = jnp.exp(final)

    @pl.when(c > 0)
    def _():
        tail.wait_recv()

    def conv(first, taps):
        width = taps.shape[1]
        total = jnp.zeros((TOK, width), F32)
        for j in range(CONV):
            total = total + taps[j : j + 1, :] * ext[5 + j : 5 + j + TOK, first : first + width]
        return total

    x_pre = conv(0, conv_x)
    x_conv = silu(x_pre)
    b_conv = silu(conv(HD, conv_b))
    c_conv = silu(conv(2 * HD, conv_c))
    b_t = b_conv.T
    read = [c_conv[:, h * HD : (h + 1) * HD] for h in range(PER)]
    driven = [steps[h] * x_conv for h in range(PER)]
    for h in range(PER):
        local_state[h] = exact(b_t, to_end[h] * driven[h])

    first_of = pl.ds(2 * k, 2)
    first_other = pl.ds(2 * (1 - k), 2)

    def scan(way, state):
        moves = [go(state.at[first_other], csib.at[way], cs.at[0, way], cs.at[1, way], sibling)]
        if way == 0:
            moves.append(go(dec, dsib, cs.at[0, 2], cs.at[1, 2], sibling))
        yield
        for move in moves:
            move.wait_recv()
        d_mine = [jnp.where(k == 0, dec[h : h + 1], dec[2 + h : 3 + h]) for h in range(2)]
        d_other = [jnp.where(k == 0, dsib[h : h + 1], dsib[2 + h : 3 + h]) for h in range(2)]
        d_chip = [d_mine[h] * d_other[h] for h in range(2)]
        nearer_is_mine = (k == 1) if way == 0 else (k == 0)
        own, theirs = state[first_of], csib[way]
        for h in range(2):
            near = jnp.where(nearer_is_mine, own[h], theirs[h])
            far = jnp.where(nearer_is_mine, theirs[h], own[h])
            d_near = jnp.where(nearer_is_mine, d_mine[h], d_other[h])
            chip = far * d_near + near
            for i in range(4):
                zsend[way, h * 4 + i, :32] = chip[i * 32 : (i + 1) * 32]
                zsend[way, h * 4 + i, 32:] = jnp.broadcast_to(d_chip[h], (8, HD))
        moves = []
        for d in range(1, NZ):
            there = lax.rem(z + d, NZ)
            moves.append(
                go(
                    zsend.at[way, there], zrecv.at[way, z],
                    zs.at[0, way, d - 1], zs.at[1, way, d - 1], z_peers[d - 1],
                )
            )
        zrecv[way, z] = zsend[way, z]
        for move in moves:
            move.wait_recv()
        along = range(NZ) if way == 0 else range(NZ - 1, -1, -1)
        total, decay = jnp.zeros((32, HD), F32), jnp.ones((1, HD), F32)
        for i in along:
            d_i = zrecv[way, i, 32:33]
            total, decay = d_i * total + zrecv[way, i, :32], decay * d_i
        xsend[way, :32] = total
        xsend[way, 32:] = jnp.broadcast_to(decay, (8, HD))
        moves = [
            go(
                xsend.at[way], xrecv.at[way, x],
                xs_.at[0, way, d - 1], xs_.at[1, way, d - 1], x_peers[d - 1],
            )
            for d in range(1, NX)
        ]
        xrecv[way, x] = xsend[way]
        for move in moves:
            move.wait_recv()
        enters = jnp.zeros((32, HD), F32)
        for i in range(NX) if way == 0 else range(NX - 1, -1, -1):
            passed = (i < x) if way == 0 else (i > x)
            enters = jnp.where(passed, xrecv[way, i, 32:33] * enters + xrecv[way, i, :32], enters)
        for i in along:
            zbs[way, i] = enters
            enters = zrecv[way, i, 32:33] * enters + zrecv[way, i, :32]
        moves = []
        for d in range(1, NZ):
            there = lax.rem(z + d, NZ)
            moves.append(
                go(
                    zbs.at[way, there], zbr.at[way, z],
                    bs.at[0, way, d - 1], bs.at[1, way, d - 1], z_peers[d - 1],
                )
            )
        zbr[way, z] = zbs[way, z]
        for move in moves:
            move.wait_recv()
        for h in range(2):
            entering = zbr[way, 4 * h : 4 * h + 4].reshape(HD, HD)
            mine_first = (k == 0) if way == 0 else (k == 1)
            d_first = jnp.where(mine_first, d_mine[h], d_other[h])
            s_first = jnp.where(mine_first, own[h], theirs[h])
            second = d_first * entering + s_first
            inc[way, 2 * k + h] = jnp.where(mine_first, entering, second)
            cback[way, h] = jnp.where(mine_first, second, entering)
        move = go(cback.at[way], inc.at[way, first_of], ks.at[0, way], ks.at[1, way], sibling)
        yield
        move.wait_recv()
        yield

    forward = scan(0, local_state)
    next(forward)
    inner = []
    for h in range(PER):
        mix[h] = exact(read[h], b_t) * within[h]
        inner.append(exact(mix[h], driven[h]) + skip_gain[:, h : h + 1] * x_conv)
    next(forward)
    next(forward)
    for h in range(PER):
        student = inner[h] + growth[h] * exact(read[h], inc[0, h])
        at = slice(h * HD, (h + 1) * HD)
        out_s[:, at] = student.astype(BF16)
        up[h] = 2.0 * (student - target[:, at]) / (HEAD_TOTAL * HD)
        sgrad[h] = exact((growth[h] * read[h]).T, up[h])

    backward = scan(1, sgrad)
    next(backward)
    x_grad = jnp.zeros((TOK, HD), F32)
    for h in range(PER):
        x_grad = x_grad + steps[h] * exact(mix[h].T, up[h]) + skip_gain[:, h : h + 1] * up[h]
    next(backward)
    next(backward)
    for h in range(PER):
        x_grad = x_grad + steps[h] * to_end[h] * exact(b_conv, inc[1, h])
    sigma = 1.0 / (1.0 + jnp.exp(-x_pre))
    ext2[:TOK] = x_grad * sigma * (1.0 + x_pre * (1.0 - sigma))
    head = remote(ext2.at[pl.ds(0, 8)], ext2.at[pl.ds(TOK, 8)], halo.at[2], halo.at[3], previous)

    @pl.when(c > 0)
    def _():
        head.start()

    @pl.when(c == last)
    def _():
        ext2[TOK:] = jnp.zeros((8, HD), F32)

    @pl.when(c < last)
    def _():
        head.wait_recv()

    grad = jnp.zeros((TOK, HD), F32)
    for j in range(CONV):
        grad = grad + conv_x[j : j + 1, :] * ext2[CONV - 1 - j : CONV - 1 - j + TOK]
    here = ig.at[pl.ds(pl.multiple_of(x * TOK, TOK), TOK)]
    here[...] = grad.astype(BF16)
    moves = [
        go(here, here, igs.at[0, d - 1], igs.at[1, d - 1], x_peers[d - 1]) for d in range(1, NX)
    ]
    for move in moves:
        move.wait_recv()
    for e in range(2):
        product = lax.dot_general(
            hidq[e], ig[...], (((0,), (0,)), ((), ())), preferred_element_type=F32
        )
        part[4 * e : 4 * e + 4] = product.reshape(4, NK, 64, HD)
    go(part.at[:, 1 - k], wrecv, wc.at[0], wc.at[1], sibling).wait_recv()
    for i in range(NZ):
        wsend[i] = part[i, k] + wrecv[i]
    moves = []
    for d in range(1, NZ):
        there = lax.rem(z + d, NZ)
        moves.append(go(wsend.at[there], wzr.at[z], wz.at[0, d - 1], wz.at[1, d - 1], z_peers[d - 1]))
    wzr[z] = wsend[z]
    for move in moves:
        move.wait_recv()
    total = wzr[0]
    for i in range(1, NZ):
        total = total + wzr[i]
    out_w[...] = total

    for move in sent:
        move.wait_send()

    @pl.when(c < last)
    def _():
        tail.wait_send()

    @pl.when(c > 0)
    def _():
        head.wait_send()


def shape(dims, dtype=F32):
    return jax.ShapeDtypeStruct(dims, dtype)


def dma(*dims):
    return pltpu.SemaphoreType.DMA(dims)


def call(kernel, collective, outs, scratch, args, limit):
    return pl.pallas_call(
        kernel,
        out_shape=outs,
        in_specs=[pl.BlockSpec(memory_space=pltpu.VMEM)] * len(args),
        out_specs=[pl.BlockSpec(memory_space=pltpu.VMEM)] * len(outs),
        scratch_shapes=scratch,
        compiler_params=pltpu.CompilerParams(
            collective_id=collective, has_side_effects=True, vmem_limit_bytes=limit
        ),
    )(*args)


def local(
    query_proj, keyval_proj, hidden, weight_x, conv_x, conv_b, conv_c, step_size, decay_log, skip_gain
):
    vm = pltpu.VMEM
    target, q_loc, k_loc, xin, hidq = call(
        front,
        0,
        (
            shape((TOK, PER * HD)), shape((TOK, PER * HD), BF16), shape((TOK, HD), BF16),
            shape((TOK, HD), BF16), shape((2, NX * TOK, 512), BF16),
        ),
        [
            vm((2, TOK, PER * HD), BF16), vm((NZ, NX, TOK, 2 * HD), BF16), vm((NM, TOK, 512), BF16),
            vm((2, PER * TOK, HD), BF16), vm((2, PER * TOK, HD), F32), vm((2, PER * TOK, HD), F32),
            vm((2, PER * TOK, HD), F32), vm((PER * TOK, HD), F32), vm((PER * TOK, HD), F32),
            vm((PER * TOK, HD), F32),
            dma(3), dma(2, 7), dma(2, 7), dma(2, 7), dma(2, 3), dma(2, 32), dma(2), dma(2, 2), dma(2, 6),
        ],
        (query_proj, keyval_proj.reshape(16, KV * 2 * HD), hidden, weight_x),
        40 * 2**20,
    )
    student, weight_grad = call(
        back,
        1,
        (shape((TOK, PER * HD), BF16), shape((64, HD))),
        [
            vm((TOK + 8, 6 * HD), F32), vm((TOK + 8, HD), F32), vm((PER, TOK, TOK), F32),
            vm((PER, HD, HD), F32), vm((PER, HD, HD), F32), vm((2, 2, HD, HD), F32),
            vm((8, HD), F32), vm((8, HD), F32),
            vm((2, NZ, 40, HD), F32), vm((2, NZ, 40, HD), F32), vm((2, 40, HD), F32), vm((2, NX, 40, HD), F32),
            vm((2, NZ, 32, HD), F32), vm((2, NZ, 32, HD), F32), vm((2, 2, HD, HD), F32),
            vm((2, PER, HD, HD), F32), vm((NX * TOK, HD), BF16), vm((NZ, NK, 64, HD), F32),
            vm((NZ, 64, HD), F32), vm((NZ, 64, HD), F32), vm((NZ, 64, HD), F32), vm((PER, TOK, HD), F32),
            dma(4), dma(2, 3), dma(2, 2, 7), dma(2, 2, 3), dma(2, 2, 7), dma(2, 2), dma(2, 3), dma(2), dma(2, 7),
        ],
        (
            xin, k_loc, q_loc, target, step_size, decay_log.reshape(1, PER), skip_gain.reshape(1, PER),
            conv_x, conv_b, conv_c, hidq,
        ),
        40 * 2**20,
    )
    return student, weight_grad


def solution(mesh):
    finer = Mesh(mesh.devices.reshape(NX, NZ, NK, mesh.shape["mp"]), CTX_MP)
    placed = (
        P(CTX_MP, None),
        P(CTX_MP, None, None),
        P(CTX, "mp"),
        P(None, "mp"),
        P(None, "mp"),
        P(None, "mp"),
        P(None, "mp"),
        P(CTX, "mp"),
        P("mp"),
        P("mp"),
    )
    return jax.shard_map(
        local, mesh=finer, in_specs=placed, out_specs=(P(CTX, "mp"), P(CTX, "mp")), check_vma=False
    )
```

time: 470 us -> 135 us (0.29)
  the two profiles are of different devices: /device:TPU:1 before, /device:TPU:9 now
where the time goes in v1:
time: 135 us
  Pallas kernels  129 us (96%)
  local copies, waits for them, and re-layouts  5.08 us (4%)
    pallas_call x2, Pallas kernels, call(): pl.pallas_call(kernel, out_shape=outs, in_specs=[pl.BlockSpec(memory_spac...  129 us
    unnamed x22, local copies, waits for them, and re-layouts  5.08 us

profile of v1, /device:TPU:9, one launch (start us, length us, event | category | flops | bytes accessed | tf_op | source)
XLA Modules:
  0.0 135.2 jit_solution(16725605729691992864)
XLA Ops:
  0.6 0.0 copy-start.1
  0.6 0.0 copy-start.8
  0.6 0.9 copy.13
  1.5 0.0 copy-done.8
  1.6 0.1 copy.12.step_size
  1.7 0.0 copy-done.1
  1.7 0.0 copy-start
  1.7 1.2 copy-done
  2.9 0.0 copy-start.2
  2.9 0.9 copy-done.2
  3.8 0.0 copy-start.4
  3.8 0.0 copy-start.5
  3.8 66.6 %shard_map.113 = (f32[128,512]{1,0:T(8,128)S(1)}, bf16[128,512]{1,0:T(8,128)(2,1)S(1)}, bf16[128,128]{1,0:T(8,128)(2,1)S(1)}, bf16[128,128]{1,0:T(8,128)(2,1)S(1)}, bf16[2,512,512]{2,1,0:T(8,128)(2,1)S(1)}) custom-call(bf16[16,4096]{1,0:T(8,128)(2,1)S(1)} %copy-done.1, bf16[16,2048]{1,0:T(8,128)(2,1)S(1)} %bitcast.4, bf16[128,512]{1,0:T(8,128)(2,1)S(1)} %copy-done.2, ...), custom_call_target="tpu_custom_call" | custom-call | tf_op jit(solution)/shard_map/pallas_call | solution.py:520
  70.4 0.0 copy-start.3
  70.4 0.0 copy-start.6
  70.4 0.0 copy-start.7
  70.4 0.0 copy-done.4
  70.4 0.0 copy-done.5
  70.5 0.6 copy-done.3
  71.1 0.0 copy-done.6
  71.1 0.0 copy-done.7
  71.1 62.9 %shard_map.114 = (bf16[128,512]{1,0:T(8,128)(2,1)S(1)}, f32[64,128]{1,0:T(8,128)S(1)}) custom-call(bf16[128,128]{1,0:T(8,128)(2,1)S(1)} %get-tuple-element.7.xin, bf16[128,128]{1,0:T(8,128)(2,1)S(1)} %get-tuple-element.8.k_loc, bf16[128,512]{1,0:T(8,128)(2,1)S(1)} %get-tuple-element.9.q_loc, f32[128,512]{1,0:T(8,128)S(1)} %get-tuple-element.10.target, ...), custom_call_target="tpu_custom_call" | custom-call | tf_op jit(solution)/shard_map/pallas_call | solution.py:520
  134.0 0.7 copy.16
  134.6 0.6 copy.17
Async XLA Ops:
  0.6 1.0 copy-start.1
  0.6 0.9 copy-start.8
  1.7 1.2 copy-start
  2.9 0.9 copy-start.2
  3.8 66.6 %copy-start.4 = (f32[4,128]{1,0:T(4,128)S(1)}, f32[4,128]{1,0:T(4,128)}, u32[]{:S(2)}) copy-start(f32[4,128]{1,0:T(4,128)} %conv_x.1) | copy-start | bytes 6148
  3.8 66.6 %copy-start.5 = (f32[4,128]{1,0:T(4,128)S(1)}, f32[4,128]{1,0:T(4,128)}, u32[]{:S(2)}) copy-start(f32[4,128]{1,0:T(4,128)} %conv_b.1) | copy-start | bytes 6148
  70.4 0.7 copy-start.3
  70.4 0.7 copy-start.6
  70.4 0.7 copy-start.7

commit v2 on v0

v2 whole, which is shorter than its diff:
```python
import types

import jax
import jax.numpy as jnp
from jax import lax
from jax.experimental import pallas as pl
from jax.experimental.pallas import tpu as pltpu
from jax.sharding import Mesh
from jax.sharding import PartitionSpec as P

HEAD_TOTAL = 32
KV = 8
HD = 128
CONV = 4
TOK = 128
PER = HEAD_TOTAL // KV
NX, NZ, NK, NM = 4, 8, 2, 8
CHIPS = NX * NZ
LAST = CHIPS * NK - 1
CTX = ("ctx_0", "ctx_1", "ctx_2")
CTX_MP = ("ctx_0", "ctx_1", "ctx_2", "mp")
MESH = pl.DeviceIdType.MESH
F32, BF16 = jnp.float32, jnp.bfloat16
NEG = -1e30
SCALE2 = HD**-0.5 * 1.4426950408889634
OFFSETS = sorted(
    ((a, b) for a in range(NX) for b in range(NZ) if a or b),
    key=lambda ab: -(min(ab[0], NX - ab[0]) + min(ab[1], NZ - ab[1])),
)


def place():
    return tuple(lax.axis_index(name) for name in CTX_MP)


def remote(src, dst, send, recv, device):
    return pltpu.make_async_remote_copy(
        src_ref=src, dst_ref=dst, send_sem=send, recv_sem=recv, device_id=device, device_id_type=MESH
    )


def greet(devices):
    barrier = pltpu.get_barrier_semaphore()
    for device in devices:
        pl.semaphore_signal(barrier, inc=1, device_id=device, device_id_type=MESH)
    pl.semaphore_wait(barrier, len(devices))


def exact(a, b, dims=((1,), (0,))):
    return lax.dot_general(
        a, b, (dims, ((), ())), precision=lax.Precision.HIGHEST, preferred_element_type=F32
    )


def silu(v):
    return v / (1.0 + jnp.exp(-v))


def dma(*dims):
    return pltpu.SemaphoreType.DMA(dims)


def scratch():
    vm = pltpu.VMEM
    return {
        "q2": vm((2, TOK, PER * HD), BF16),
        "kvb": vm((NZ, NX, TOK, 2 * HD), BF16),
        "hall": vm((NM, TOK, 512), BF16),
        "hidq": vm((2, NX * TOK, 512), BF16),
        "qs": vm((2, PER * TOK, HD), BF16),
        "m_s": vm((2, PER * TOK, HD), F32),
        "l_s": vm((2, PER * TOK, HD), F32),
        "acc": vm((2, PER * TOK, HD), F32),
        "stat": vm((PER * TOK, HD), F32),
        "acc_in": vm((PER * TOK, HD), F32),
        "stat_in": vm((PER * TOK, HD), F32),
        "target": vm((PER, TOK, HD), F32),
        "ext": vm((TOK + 8, 6 * HD), F32),
        "ext2": vm((TOK + 8, HD), F32),
        "growth": vm((PER, TOK, TOK), F32),
        "to_end": vm((PER, TOK, TOK), F32),
        "within": vm((PER, TOK, TOK), F32),
        "mix": vm((PER, TOK, TOK), F32),
        "read": vm((PER, TOK, HD), F32),
        "inner": vm((PER, TOK, HD), F32),
        "up": vm((PER, TOK, HD), F32),
        "bconv": vm((TOK, HD), F32),
        "xconv": vm((TOK, HD), F32),
        "xpre": vm((TOK, HD), F32),
        "state": vm((2, PER, HD, HD), F32),
        "csib": vm((2, 2, HD, HD), F32),
        "cback": vm((2, 2, HD, HD), F32),
        "inc": vm((2, PER, HD, HD), F32),
        "dec": vm((8, HD), F32),
        "dsib": vm((8, HD), F32),
        "dsend": vm((2, 8, HD), F32),
        "drecv": vm((CHIPS, 8, HD), F32),
        "zsend": vm((2, CHIPS, 8, HD), F32),
        "zrecv": vm((2, CHIPS, 8, HD), F32),
        "zbs": vm((2, CHIPS, 8, HD), F32),
        "zbr": vm((2, CHIPS, 8, HD), F32),
        "ig": vm((NX * TOK, HD), BF16),
        "part": vm((NZ, NK, 64, HD), F32),
        "wrecv": vm((NZ, 64, HD), F32),
        "wsend": vm((NZ, 64, HD), F32),
        "wzr": vm((NZ, 64, HD), F32),
        "own_s": dma(3),
        "yq": dma(2, 7),
        "ykv": dma(2, 7),
        "yh": dma(2, 7),
        "xkv": dma(2, NX),
        "xf": dma(2, NX * NZ),
        "ring": dma(2, 32),
        "cq": dma(2),
        "co": dma(2, 2),
        "hq": dma(2, 6),
        "halo": dma(2, 3),
        "cs": dma(2, 3),
        "ds": dma(2, 31),
        "zs": dma(2, 62),
        "bs": dma(2, 62),
        "ks": dma(2, 2),
        "igs": dma(2, 3),
        "wc": dma(2),
        "wz": dma(2, 7),
    }


def layer(
    q_in, kv_in, hid_in, wx, step_size, decay_log, skip_gain, conv_x, conv_b, conv_c, out_s, out_w, *rest
):
    r = types.SimpleNamespace(**dict(zip(scratch(), rest, strict=True)))
    x, z, k, m = place()
    chip = x * NZ + z
    c = chip * NK + k
    sibling = (x, z, 1 - k, m)
    zr, zl = lax.rem(z + 1, NZ), lax.rem(z + NZ - 1, NZ)
    y_peers = [(x, z, k, lax.rem(m + d, NM)) for d in range(1, NM)]
    x_peers = [(lax.rem(x + d, NX), z, k, m) for d in range(1, NX)]
    z_peers = [(x, lax.rem(z + d, NZ), k, m) for d in range(1, NZ)]
    plane = [(lax.rem(x + a, NX), lax.rem(z + b, NZ), k, m) for a, b in OFFSETS]

    def at_ctx(i):
        return (lax.div(i, NZ * NK), lax.rem(lax.div(i, NK), NZ), lax.rem(i, NK), m)

    following, previous = at_ctx(lax.rem(c + 1, LAST + 1)), at_ctx(lax.rem(c + LAST, LAST + 1))
    greet([*y_peers, *plane, sibling, following, previous])
    sent = []

    def go(*args):
        move = remote(*args)
        move.start()
        sent.append(move)
        return move

    def arrived(moves):
        for move in moves:
            move.wait_recv()

    rows = pl.ds(pl.multiple_of(m * 16, 16), 16)

    def columns(i, width):
        return pl.ds(pl.multiple_of(i * width, width), width)

    kv_moves = [
        go(kv_in.at[:, columns(p[3], 256)], r.kvb.at[z, x, rows], r.ykv.at[0, d], r.ykv.at[1, d], p)
        for d, p in enumerate(y_peers)
    ]
    q_moves = [
        go(q_in.at[:, columns(p[3], 512)], r.q2.at[0, rows], r.yq.at[0, d], r.yq.at[1, d], p)
        for d, p in enumerate(y_peers)
    ]
    h_moves = [
        go(hid_in, r.hall.at[m], r.yh.at[0, d], r.yh.at[1, d], p) for d, p in enumerate(y_peers)
    ]
    mine = [
        pltpu.make_async_copy(kv_in.at[:, columns(m, 256)], r.kvb.at[z, x, rows], r.own_s.at[0]),
        pltpu.make_async_copy(q_in.at[:, columns(m, 512)], r.q2.at[0, rows], r.own_s.at[1]),
        pltpu.make_async_copy(hid_in, r.hall.at[m], r.own_s.at[2]),
    ]
    for move in mine:
        move.start()

    row = lax.broadcasted_iota(jnp.int32, (TOK, TOK), 0)
    col = lax.broadcasted_iota(jnp.int32, (TOK, TOK), 1)
    causal = row >= col
    lower = jnp.where(causal, 1.0, 0.0)
    rate = -jnp.exp(decay_log[...])

    def step_of(h):
        return jnp.broadcast_to(step_size[:, h : h + 1], (TOK, HD))

    for h in range(PER):
        log_decay = exact(lower, step_of(h) * rate[:, h : h + 1])
        final = log_decay[TOK - 1 :]
        r.growth[h] = jnp.exp(log_decay)
        r.to_end[h] = jnp.exp(final - log_decay)
        r.within[h] = jnp.where(
            causal, jnp.exp(jnp.where(causal, log_decay - log_decay.T, 0.0)), 0.0
        )
        r.dec[h : h + 1] = jnp.exp(final)
        r.dec[PER + h : PER + h + 1] = jnp.exp(final)
    d_move = go(r.dec, r.dsib, r.cs.at[0, 2], r.cs.at[1, 2], sibling)

    for xs in range(1, NX):

        @pl.when(xs > x)
        def _(xs=xs):
            r.kvb[:, xs] = jnp.zeros((NZ, TOK, 2 * HD), BF16)

    r.m_s[...] = jnp.full(r.m_s.shape, NEG, F32)
    r.l_s[...] = jnp.zeros(r.l_s.shape, F32)
    r.acc[...] = jnp.zeros(r.acc.shape, F32)

    def in_ring(xs):
        return (x == xs) | (x == xs + 2) | ((x == 1) & (xs == 0))

    def by_x(xs):
        return (x == 3 - xs) if xs < 2 else (x == 3) & (xs == 2)

    def ring_copy(way, step, xs):
        if way == 0:
            column, device = lax.rem(z - (step - 1) + NZ, NZ), (x, zr, k, m)
        else:
            column, device = lax.rem(z + (step - 1), NZ), (x, zl, k, m)
        slot = r.kvb.at[column, xs]
        at = (way * 4 + step - 1) * NX + xs
        return remote(slot, slot, r.ring.at[0, at], r.ring.at[1, at], device)

    def first_copy(xs, to):
        slot = r.kvb.at[z, xs]
        return remote(slot, slot, r.xkv.at[0, to], r.xkv.at[1, to], (to, z, k, m))

    FIRST = ((0, 1), (0, 2), (1, 3))

    def across(column, xs):
        to = (3, 2, 3)[xs]
        slot, at = r.kvb.at[column, xs], xs * NZ + column
        return remote(slot, slot, r.xf.at[0, at], r.xf.at[1, at], (to, z, k, m))

    for move in mine:
        move.wait()
    arrived(kv_moves)
    for xs in range(NX):

        @pl.when(x == xs)
        def _(xs=xs):
            for source, to in FIRST:
                if source == xs:
                    first_copy(xs, to).start()
            ring_copy(0, 1, xs).start()
            ring_copy(1, 1, xs).start()
            if xs < 3:
                across(z, xs).start()

    d_move.wait_recv()
    for h in range(2):
        chip_decay = r.dec[...] * r.dsib[...]
        decay_row = jnp.where(k == 0, chip_decay[h : h + 1], chip_decay[2 + h : 3 + h])
        r.dsend[h] = jnp.broadcast_to(decay_row, (8, HD))
    decay_moves = [
        go(r.dsend.at[lax.div(p[0], 2)], r.drecv.at[chip], r.ds.at[0, i], r.ds.at[1, i], p)
        for i, p in enumerate(plane)
    ]
    r.drecv[chip] = r.dsend[lax.div(x, 2)]

    arrived(q_moves)
    cq_move = go(r.q2.at[0], r.q2.at[1], r.cq.at[0], r.cq.at[1], sibling)
    for source, to in FIRST:

        @pl.when(x == to)
        def _(source=source, to=to):
            first_copy(source, to).wait_recv()
            ring_copy(0, 1, source).start()
            ring_copy(1, 1, source).start()

    r.ext[8:, HD : 2 * HD] = r.kvb[z, x, :, :HD].astype(F32)
    r.ext[8:, 2 * HD :] = r.q2[0].astype(F32)

    def tail(i):
        at = pl.ds(HD, 5 * HD) if i == 0 else pl.ds(0, HD)
        return remote(
            r.ext.at[pl.ds(TOK, 8), at], r.ext.at[pl.ds(0, 8), at],
            r.halo.at[0, i], r.halo.at[1, i], following,
        )

    @pl.when(c < LAST)
    def _():
        tail(0).start()

    @pl.when(c == 0)
    def _():
        r.ext[:8] = jnp.zeros((8, 6 * HD), F32)

    for h in range(PER):
        r.qs[0, h * TOK : (h + 1) * TOK] = r.q2[0, :, h * HD : (h + 1) * HD]
    cq_move.wait_recv()
    for h in range(PER):
        r.qs[1, h * TOK : (h + 1) * TOK] = r.q2[1, :, h * HD : (h + 1) * HD]

    def attend(column, masked):
        for xs in range(NX - 1):

            @pl.when(by_x(xs))
            def _(xs=xs):
                across(column, xs).wait_recv()

        def tile(i, carry):
            side, first = lax.div(i, 2), pl.multiple_of(lax.rem(i, 2) * 256, 256)
            at = pl.ds(first, 256)
            block = r.kvb[column].reshape(NX * TOK, 2 * HD)
            s = lax.dot_general(
                r.qs[side, at], block[:, :HD], (((1,), (1,)), ((), ())), preferred_element_type=F32
            )
            if masked:
                key = lax.broadcasted_iota(jnp.int32, (256, NX * TOK), 1)
                query = lax.broadcasted_iota(jnp.int32, (256, NX * TOK), 0)
                core = jnp.where(side == 0, k, 1 - k)
                ahead = (key - x * TOK) + k * TOK - (lax.rem(query, TOK) + core * TOK)
                allowed = (key < x * TOK) | ((ahead <= 0) & (key < (x + 1) * TOK))
                s = jnp.where(allowed, s * SCALE2, NEG)
            else:
                key = lax.broadcasted_iota(jnp.int32, (1, NX * TOK), 1)
                limit = jnp.where(column < z, (x + 1) * TOK, x * TOK)
                s = s * SCALE2 + jnp.where(key < limit, 0.0, NEG)
            before = r.m_s[side, at, :1]
            now = jnp.maximum(before, jnp.max(s, axis=1, keepdims=True))
            p = jnp.exp2(s - now)
            alpha = jnp.exp2(before - now)
            r.m_s[side, at] = jnp.broadcast_to(now, (256, HD))
            r.l_s[side, at] = r.l_s[side, at] * alpha + jnp.sum(p, axis=1, keepdims=True)
            r.acc[side, at] = r.acc[side, at] * alpha + jnp.dot(
                p.astype(BF16), block[:, HD:], preferred_element_type=F32
            )
            return carry

        lax.fori_loop(0, 4, tile, 0)

    def receive(step):
        for way in range(2):
            if way == 1 and step == 4:
                continue
            column = lax.rem(z - step + NZ, NZ) if way == 0 else lax.rem(z + step, NZ)
            for xs in range(NX):

                @pl.when(in_ring(xs))
                def _(way=way, xs=xs):
                    ring_copy(way, step, xs).wait_recv()
                    if step < (4, 3)[way]:
                        ring_copy(way, step + 1, xs).start()
                    if xs < 3:

                        @pl.when(x == xs)
                        def _():
                            across(column, xs).start()

    def right(step):
        return lax.rem(z - step + NZ, NZ)

    def left(step):
        return lax.rem(z + step, NZ)

    def conv(first, taps):
        width = taps.shape[1]
        total = jnp.zeros((TOK, width), F32)
        for j in range(CONV):
            total = total + taps[j : j + 1, :] * r.ext[5 + j : 5 + j + TOK, first : first + width]
        return total

    def readouts():
        @pl.when(c > 0)
        def _():
            tail(0).wait_recv()

        b_conv = silu(conv(HD, conv_b))
        r.bconv[...] = b_conv
        c_conv = silu(conv(2 * HD, conv_c))
        b_t = b_conv.T
        for h in range(PER):
            read = c_conv[:, h * HD : (h + 1) * HD]
            r.read[h] = read
            r.mix[h] = exact(read, b_t) * r.within[h]

    def project():
        arrived(h_moves)
        total = jnp.zeros((TOK, HD), F32)
        for j in range(NM):
            total = total + jnp.dot(
                r.hall[j], wx[j * 512 : (j + 1) * 512], preferred_element_type=F32
            )
        r.ext[8:, :HD] = total.astype(BF16).astype(F32)

        @pl.when(c < LAST)
        def _():
            tail(1).start()

        moves = []
        for d in range(1, NX):
            there = lax.rem(x + d, NX)
            for e in range(2):
                at = (d - 1) * 2 + e
                into = r.hidq.at[e, columns(x, TOK)]
                moves.append(
                    go(r.hall.at[2 * there + e], into, r.hq.at[0, at], r.hq.at[1, at], x_peers[d - 1])
                )
        for e in range(2):
            r.hidq[e, columns(x, TOK)] = r.hall[2 * x + e]
        return moves

    def states():
        @pl.when(c > 0)
        def _():
            tail(1).wait_recv()

        x_pre = conv(0, conv_x)
        x_conv = silu(x_pre)
        r.xpre[...] = x_pre
        r.xconv[...] = x_conv
        b_t = r.bconv[...].T
        for h in range(PER):
            r.state[0, h] = exact(b_t, r.to_end[h] * (step_of(h) * x_conv))

    def inners():
        x_conv = r.xconv[...]
        for h in range(PER):
            r.inner[h] = exact(r.mix[h], step_of(h) * x_conv) + skip_gain[:, h : h + 1] * x_conv

    first_of, first_other = pl.ds(2 * k, 2), pl.ds(2 * (1 - k), 2)

    def scan(way):
        state = r.state.at[way]
        move = go(state.at[first_other], r.csib.at[way], r.cs.at[0, way], r.cs.at[1, way], sibling)
        yield
        move.wait_recv()
        d_mine = [jnp.where(k == 0, r.dec[h : h + 1], r.dec[2 + h : 3 + h]) for h in range(2)]
        d_other = [jnp.where(k == 0, r.dsib[h : h + 1], r.dsib[2 + h : 3 + h]) for h in range(2)]
        mine_first = (k == 0) if way == 0 else (k == 1)
        for h in range(2):
            own, theirs = state[2 * k + h], r.csib[way, h]
            near = jnp.where(mine_first, theirs, own)
            far = jnp.where(mine_first, own, theirs)
            d_near = jnp.where(mine_first, d_other[h], d_mine[h])
            both = far * d_near + near
            r.zsend[way, 16 * h : 16 * h + 16] = both.reshape(16, 8, HD)
        moves = []
        for i, p in enumerate(plane):
            at = way * 31 + i
            there = p[0] * NZ + p[1]
            moves.append(
                go(r.zsend.at[way, there], r.zrecv.at[way, chip], r.zs.at[0, at], r.zs.at[1, at], p)
            )
        r.zrecv[way, chip] = r.zsend[way, chip]
        yield
        arrived(moves)
        enters = jnp.zeros((8, HD), F32)
        for j in range(CHIPS) if way == 0 else range(CHIPS - 1, -1, -1):
            r.zbs[way, j] = enters
            enters = r.drecv[j] * enters + r.zrecv[way, j]
        moves = []
        for i, p in enumerate(plane):
            at = way * 31 + i
            there = p[0] * NZ + p[1]
            moves.append(
                go(r.zbs.at[way, there], r.zbr.at[way, chip], r.bs.at[0, at], r.bs.at[1, at], p)
            )
        r.zbr[way, chip] = r.zbs[way, chip]
        yield
        arrived(moves)
        for h in range(2):
            entering = r.zbr[way, 16 * h : 16 * h + 16].reshape(HD, HD)
            own, theirs = state[2 * k + h], r.csib[way, h]
            d_first = jnp.where(mine_first, d_mine[h], d_other[h])
            second = d_first * entering + jnp.where(mine_first, own, theirs)
            r.inc[way, 2 * k + h] = jnp.where(mine_first, entering, second)
            r.cback[way, h] = jnp.where(mine_first, second, entering)
        move = go(r.cback.at[way], r.inc.at[way, first_of], r.ks.at[0, way], r.ks.at[1, way], sibling)
        yield
        move.wait_recv()
        yield

    receive(1)
    attend(z, True)
    readouts()
    receive(2)
    attend(right(1), False)
    attend(left(1), False)
    receive(3)
    attend(right(2), False)
    attend(left(2), False)
    receive(4)
    hq_moves = project()
    attend(right(3), False)
    states()
    arrived(decay_moves)
    forward = scan(0)
    next(forward)
    inners()
    next(forward)
    attend(left(3), False)
    attend(right(4), False)
    lane = lax.broadcasted_iota(jnp.int32, (PER * TOK, HD), 1)
    r.stat[...] = jnp.where(lane < 64, r.m_s[1], r.l_s[1])
    o_moves = [
        go(r.acc.at[1], r.acc_in, r.co.at[0, 0], r.co.at[1, 0], sibling),
        go(r.stat, r.stat_in, r.co.at[0, 1], r.co.at[1, 1], sibling),
    ]
    next(forward)
    arrived(o_moves)
    other, mine_max = r.stat_in[:, :1], r.m_s[0, :, :1]
    both = jnp.maximum(other, mine_max)
    a0, a1 = jnp.exp2(mine_max - both), jnp.exp2(other - both)
    norm = r.l_s[0, :, :1] * a0 + r.stat_in[:, 64:65] * a1
    r.target[...] = ((r.acc[0] * a0 + r.acc_in[...] * a1) / norm).reshape(PER, TOK, HD)
    next(forward)
    next(forward)
    for h in range(PER):
        student = r.inner[h] + r.growth[h] * exact(r.read[h], r.inc[0, h])
        out_s[:, h * HD : (h + 1) * HD] = student.astype(BF16)
        r.up[h] = 2.0 * (student - r.target[h]) / (HEAD_TOTAL * HD)
        r.state[1, h] = exact((r.growth[h] * r.read[h]).T, r.up[h])

    backward = scan(1)
    next(backward)
    next(backward)
    x_grad = jnp.zeros((TOK, HD), F32)
    for h in range(PER):
        up = r.up[h]
        x_grad = x_grad + step_of(h) * exact(r.mix[h].T, up) + skip_gain[:, h : h + 1] * up
    next(backward)
    next(backward)
    next(backward)
    b_conv = r.bconv[...]
    for h in range(PER):
        x_grad = x_grad + step_of(h) * r.to_end[h] * exact(b_conv, r.inc[1, h])
    x_pre = r.xpre[...]
    sigma = 1.0 / (1.0 + jnp.exp(-x_pre))
    r.ext2[:TOK] = x_grad * sigma * (1.0 + x_pre * (1.0 - sigma))
    head = remote(
        r.ext2.at[pl.ds(0, 8)], r.ext2.at[pl.ds(TOK, 8)], r.halo.at[0, 2], r.halo.at[1, 2], previous
    )

    @pl.when(c > 0)
    def _():
        head.start()

    @pl.when(c == LAST)
    def _():
        r.ext2[TOK:] = jnp.zeros((8, HD), F32)

    @pl.when(c < LAST)
    def _():
        head.wait_recv()

    grad = jnp.zeros((TOK, HD), F32)
    for j in range(CONV):
        grad = grad + conv_x[j : j + 1, :] * r.ext2[CONV - 1 - j : CONV - 1 - j + TOK]
    here = r.ig.at[columns(x, TOK)]
    here[...] = grad.astype(BF16)
    moves = [
        go(here, here, r.igs.at[0, d], r.igs.at[1, d], p) for d, p in enumerate(x_peers)
    ]
    arrived(hq_moves)
    arrived(moves)
    for e in range(2):
        product = lax.dot_general(
            r.hidq[e], r.ig[...], (((0,), (0,)), ((), ())), preferred_element_type=F32
        )
        r.part[4 * e : 4 * e + 4] = product.reshape(4, NK, 64, HD)
    go(r.part.at[:, 1 - k], r.wrecv, r.wc.at[0], r.wc.at[1], sibling).wait_recv()
    for i in range(NZ):
        r.wsend[i] = r.part[i, k] + r.wrecv[i]
    moves = [
        go(r.wsend.at[p[1]], r.wzr.at[z], r.wz.at[0, d], r.wz.at[1, d], p)
        for d, p in enumerate(z_peers)
    ]
    r.wzr[z] = r.wsend[z]
    arrived(moves)
    total = r.wzr[0]
    for i in range(1, NZ):
        total = total + r.wzr[i]
    out_w[...] = total

    for move in sent:
        move.wait_send()

    @pl.when(c < LAST)
    def _():
        tail(0).wait_send()
        tail(1).wait_send()

    @pl.when(c > 0)
    def _():
        head.wait_send()

    for source, to in FIRST:

        @pl.when(x == source)
        def _(source=source, to=to):
            first_copy(source, to).wait_send()

    for xs in range(NX):

        @pl.when(in_ring(xs))
        def _(xs=xs):
            for way in range(2):
                for step in range(1, (4, 3)[way] + 1):
                    ring_copy(way, step, xs).wait_send()

        if xs < 3:

            @pl.when(x == xs)
            def _(xs=xs):
                for column in range(NZ):
                    across(column, xs).wait_send()


def local(
    query_proj, keyval_proj, hidden, weight_x, conv_x, conv_b, conv_c, step_size, decay_log, skip_gain
):
    args = (
        query_proj, keyval_proj.reshape(16, KV * 2 * HD), hidden, weight_x, step_size,
        decay_log.reshape(1, PER), skip_gain.reshape(1, PER), conv_x, conv_b, conv_c,
    )
    return pl.pallas_call(
        layer,
        out_shape=(
            jax.ShapeDtypeStruct((TOK, PER * HD), BF16),
            jax.ShapeDtypeStruct((64, HD), F32),
        ),
        in_specs=[pl.BlockSpec(memory_space=pltpu.VMEM)] * len(args),
        out_specs=[pl.BlockSpec(memory_space=pltpu.VMEM)] * 2,
        scratch_shapes=list(scratch().values()),
        compiler_params=pltpu.CompilerParams(
            collective_id=0, has_side_effects=True, vmem_limit_bytes=48 * 2**20
        ),
    )(*args)


def solution(mesh):
    finer = Mesh(mesh.devices.reshape(NX, NZ, NK, mesh.shape["mp"]), CTX_MP)
    placed = (
        P(CTX_MP, None),
        P(CTX_MP, None, None),
        P(CTX, "mp"),
        P(None, "mp"),
        P(None, "mp"),
        P(None, "mp"),
        P(None, "mp"),
        P(CTX, "mp"),
        P("mp"),
        P("mp"),
    )
    return jax.shard_map(
        local, mesh=finer, in_specs=placed, out_specs=(P(CTX, "mp"), P(CTX, "mp")), check_vma=False
    )
```

time: 470 us -> 111 us (0.24)
  waiting for transfers between devices: 237 us -> 0 us
  Pallas kernels: 0 us -> 104 us
  blocking collectives: 54.7 us -> 0 us
  loops' own time: 42.5 us -> 0 us
  local copies, waits for them, and re-layouts: 40.6 us -> 4.97 us
  starting transfers between devices: 31.5 us -> 0 us
  matrix products: 24.7 us -> 0 us
  other arithmetic: 22.5 us -> 0 us
  between operations: 14.8 us -> 0.72 us
    all_gather x6 -> x0, waiting for transfers between devices: 159 us -> none  [the longest x4 93.7 us: entering(): pieces = jax.tree.map(lambda part: lax.all_gather(part, axis), subtotal)]
    pallas_call x0 -> x1, Pallas kernels: none -> 104 us  [local(): pl.pallas_call(layer, out_shape=(jax.ShapeDtypeStruct((TOK, PER * HD), BF...]
    all_to_all x3 -> x0, waiting for transfers between devices: 75.4 us -> none  [the longest x1 50.4 us: sum_at_owner(): lax.all_to_all(parts, axis, split_axis=0, concat_axis=0, tiled=True)]
    all_gather x7 -> x0, blocking collectives: 54.7 us -> none  [the longest x6 38.7 us: entering(): pieces = jax.tree.map(lambda part: lax.all_gather(part, axis), subtotal)]
    another operation x1 -> x0, loops' own time: 42.5 us -> none  [local(): lax.scan(one_block, start_carry, jnp.arange(block_count, dtype=jnp.int32))]
    dot_general x41 -> x0, matrix products: 24.7 us -> none  [the longest x16 7.98 us: one_block(): jnp.einsum('gqk,kgd->gqd', weights.astype(jnp.bfloat16), key_block[:, :,...]
    all_to_all x3 -> x0, starting transfers between devices: 20.3 us -> none  [the longest x1 8.96 us: sum_at_owner(): lax.all_to_all(parts, axis, split_axis=0, concat_axis=0, tiled=True)]
    squeeze x17 -> x0, local copies, waits for them, and re-layouts: 16.1 us -> none  [the longest x16 15.6 us: one_block(): key_block = lax.dynamic_index_in_dim(blocks, block_index, 0, keepdims=False)]
  transfers between devices with their start and end apart: 11 -> 0, of which waited for: 11 -> 0; matrix products, arithmetic and copies ran while one was open for 4% -> 0% of each run, Pallas kernels for 0% -> 0%
where the time goes in v2:
time: 111 us; the launch traced here: 110 us
  Pallas kernels  104 us (94%)
  local copies, waits for them, and re-layouts  4.97 us (4%)
    pallas_call x1, Pallas kernels, local(): pl.pallas_call(layer, out_shape=(jax.ShapeDtypeStruct((TOK, PER * HD), BF...  104 us
    unnamed x22, local copies, waits for them, and re-layouts  4.97 us

profile of v2, /device:TPU:1, one launch (start us, length us, event | category | flops | bytes accessed | tf_op | source)
XLA Modules:
  0.0 110.0 jit_solution(1733450833031619257)
XLA Ops:
  0.6 0.0 copy-start.1
  0.6 0.0 copy-start.8
  0.6 0.9 copy.13
  1.5 0.0 copy-done.8
  1.6 0.0 copy-start.3
  1.6 0.0 copy-start.4
  1.6 0.0 copy-start.5
  1.6 0.0 copy-start.6
  1.6 0.0 copy-start.7
  1.6 0.1 copy.12.step_size
  1.7 0.0 copy-done.1
  1.7 0.5 copy-done.3
  2.3 0.0 copy-done.4
  2.3 0.0 copy-done.5
  2.3 0.0 copy-done.6
  2.3 0.0 copy-done.7
  2.3 0.0 copy-start
  2.3 1.2 %copy-done = bf16[4096,128]{1,0:T(8,128)(2,1)S(1)} copy-done((bf16[4096,128]{1,0:T(8,128)(2,1)S(1)}, bf16[4096,128]{1,0:T(8,128)(2,1)}, u32[]{:S(2)}) %copy-start) | copy-done | bytes 1048600
  3.5 0.0 copy-start.2
  3.5 0.9 copy-done.2
  4.4 104.3 %shard_map.113 = (bf16[128,512]{1,0:T(8,128)(2,1)S(1)}, f32[64,128]{1,0:T(8,128)S(1)}) custom-call(bf16[16,4096]{1,0:T(8,128)(2,1)S(1)} %copy-done.1, bf16[16,2048]{1,0:T(8,128)(2,1)S(1)} %bitcast.4, bf16[128,512]{1,0:T(8,128)(2,1)S(1)} %copy-done.2, bf16[4096,128]{1,0:T(8,128)(2,1)S(1)} %copy-done, f32[128,4]{1,0:T(8,128)S(1)} %copy.12.step_size, ...), custom_call_target="tpu_custom_call" | custom-call | tf_op jit(solution)/shard_map/pallas_call | solution.py:624
  108.7 0.7 copy.16
  109.4 0.6 copy.17
Async XLA Ops:
  0.6 1.1 %copy-start.1 = (bf16[16,4096]{1,0:T(8,128)(2,1)S(1)}, bf16[16,4096]{1,0:T(8,128)(2,1)}, u32[]{:S(2)}) copy-start(bf16[16,4096]{1,0:T(8,128)(2,1)} %q_in.1) | copy-start | bytes 393220
  0.6 0.9 copy-start.8
  1.6 0.7 copy-start.3
  1.6 0.7 copy-start.4
  1.6 0.7 copy-start.5
  1.6 0.7 copy-start.6
  1.6 0.7 copy-start.7
  2.3 1.2 %copy-start = (bf16[4096,128]{1,0:T(8,128)(2,1)S(1)}, bf16[4096,128]{1,0:T(8,128)(2,1)}, u32[]{:S(2)}) copy-start(bf16[4096,128]{1,0:T(8,128)(2,1)} %wx.1) | copy-start | bytes 3145732
  3.5 0.9 copy-start.2

commit v3 on v2

--- a/solution.py
+++ b/solution.py
@@ -65,7 +65,8 @@
     return {
         "q2": vm((2, TOK, PER * HD), BF16),
         "kvb": vm((NZ, NX, TOK, 2 * HD), BF16),
-        "hall": vm((NM, TOK, 512), BF16),
+        "hall": vm((NM, TOK + 16, 512), BF16),
+        "wx": vm((4096, HD), BF16),
         "hidq": vm((2, NX * TOK, 512), BF16),
         "qs": vm((2, PER * TOK, HD), BF16),
         "m_s": vm((2, PER * TOK, HD), F32),
@@ -104,17 +105,18 @@
         "wrecv": vm((NZ, 64, HD), F32),
         "wsend": vm((NZ, 64, HD), F32),
         "wzr": vm((NZ, 64, HD), F32),
-        "own_s": dma(3),
+        "own_s": dma(4),
         "yq": dma(2, 7),
         "ykv": dma(2, 7),
-        "yh": dma(2, 7),
+        "yh": dma(2, 24),
+        "ht": dma(2),
         "xkv": dma(2, NX),
         "xf": dma(2, NX * NZ),
         "ring": dma(2, 32),
         "cq": dma(2),
         "co": dma(2, 2),
         "hq": dma(2, 6),
-        "halo": dma(2, 3),
+        "halo": dma(2, 2),
         "cs": dma(2, 3),
         "ds": dma(2, 31),
         "zs": dma(2, 62),
@@ -166,19 +168,47 @@
         go(kv_in.at[:, columns(p[3], 256)], r.kvb.at[z, x, rows], r.ykv.at[0, d], r.ykv.at[1, d], p)
         for d, p in enumerate(y_peers)
     ]
+    def hidden_copy(way, step, part):
+        block = lax.rem(m - (step - 1) + NM, NM) if way == 0 else lax.rem(m + step - 1, NM)
+        peer = y_peers[0] if way == 0 else y_peers[-1]
+        at = (way * 4 + step - 1) * 3 + part
+        slot = r.hall.at[block, pl.ds((16, 80, 0)[part], (64, 64, 16)[part])]
+        source = hid_in.at[pl.ds(64 * part, 64)] if step == 1 and part < 2 else slot
+        return remote(source, slot, r.yh.at[0, at], r.yh.at[1, at], peer)
+
+    def hidden_parts(way, step):
+        return (0, 1, 2) if step < 4 else ((0, 2), (1,))[way]
+
+    def pass_on(step):
+        for part in range(3):
+            for way in range(2):
+                if part in hidden_parts(way, step):
+                    hidden_copy(way, step, part).wait_recv()
+                    if step < 4 and part in hidden_parts(way, step + 1):
+                        hidden_copy(way, step + 1, part).start()
+
+    end = remote(
+        hid_in.at[pl.ds(TOK - 16, 16)], r.hall.at[m, pl.ds(0, 16)], r.ht.at[0], r.ht.at[1], following
+    )
+
+    @pl.when(c < LAST)
+    def _():
+        end.start()
+
+    for part in range(2):
+        for way in range(2):
+            hidden_copy(way, 1, part).start()
     q_moves = [
         go(q_in.at[:, columns(p[3], 512)], r.q2.at[0, rows], r.yq.at[0, d], r.yq.at[1, d], p)
         for d, p in enumerate(y_peers)
     ]
-    h_moves = [
-        go(hid_in, r.hall.at[m], r.yh.at[0, d], r.yh.at[1, d], p) for d, p in enumerate(y_peers)
-    ]
     mine = [
         pltpu.make_async_copy(kv_in.at[:, columns(m, 256)], r.kvb.at[z, x, rows], r.own_s.at[0]),
         pltpu.make_async_copy(q_in.at[:, columns(m, 512)], r.q2.at[0, rows], r.own_s.at[1]),
-        pltpu.make_async_copy(hid_in, r.hall.at[m], r.own_s.at[2]),
+        pltpu.make_async_copy(hid_in, r.hall.at[m, pl.ds(16, TOK)], r.own_s.at[2]),
     ]
-    for move in mine:
+    wx_move = pltpu.make_async_copy(wx, r.wx, r.own_s.at[3])
+    for move in [*mine, wx_move]:
         move.start()
 
     row = lax.broadcasted_iota(jnp.int32, (TOK, TOK), 0)
@@ -253,6 +283,44 @@
             if xs < 3:
                 across(z, xs).start()
 
+    @pl.when(c > 0)
+    def _():
+        end.wait_recv()
+
+    @pl.when(c == 0)
+    def _():
+        r.hall[m, :16] = jnp.zeros((16, 512), BF16)
+
+    for way in range(2):
+        hidden_copy(way, 1, 2).start()
+    pass_on(1)
+
+    arrived(q_moves)
+    cq_move = go(r.q2.at[0], r.q2.at[1], r.cq.at[0], r.cq.at[1], sibling)
+    for source, to in FIRST:
+
+        @pl.when(x == to)
+        def _(source=source, to=to):
+            first_copy(source, to).wait_recv()
+            ring_copy(0, 1, source).start()
+            ring_copy(1, 1, source).start()
+
+    r.ext[8:, HD : 2 * HD] = r.kvb[z, x, :, :HD].astype(F32)
+    r.ext[8:, 2 * HD :] = r.q2[0].astype(F32)
+
+    at = pl.ds(HD, 5 * HD)
+    tail = remote(
+        r.ext.at[pl.ds(TOK, 8), at], r.ext.at[pl.ds(0, 8), at], r.halo.at[0, 0], r.halo.at[1, 0], following
+    )
+
+    @pl.when(c < LAST)
+    def _():
+        tail.start()
+
+    @pl.when(c == 0)
+    def _():
+        r.ext[:8, HD:] = jnp.zeros((8, 5 * HD), F32)
+
     d_move.wait_recv()
     for h in range(2):
         chip_decay = r.dec[...] * r.dsib[...]
@@ -264,36 +332,9 @@
     ]
     r.drecv[chip] = r.dsend[lax.div(x, 2)]
 
-    arrived(q_moves)
-    cq_move = go(r.q2.at[0], r.q2.at[1], r.cq.at[0], r.cq.at[1], sibling)
-    for source, to in FIRST:
-
-        @pl.when(x == to)
-        def _(source=source, to=to):
-            first_copy(source, to).wait_recv()
-            ring_copy(0, 1, source).start()
-            ring_copy(1, 1, source).start()
-
-    r.ext[8:, HD : 2 * HD] = r.kvb[z, x, :, :HD].astype(F32)
-    r.ext[8:, 2 * HD :] = r.q2[0].astype(F32)
-
-    def tail(i):
-        at = pl.ds(HD, 5 * HD) if i == 0 else pl.ds(0, HD)
-        return remote(
-            r.ext.at[pl.ds(TOK, 8), at], r.ext.at[pl.ds(0, 8), at],
-            r.halo.at[0, i], r.halo.at[1, i], following,
-        )
-
-    @pl.when(c < LAST)
-    def _():
-        tail(0).start()
-
-    @pl.when(c == 0)
-    def _():
-        r.ext[:8] = jnp.zeros((8, 6 * HD), F32)
-
     for h in range(PER):
         r.qs[0, h * TOK : (h + 1) * TOK] = r.q2[0, :, h * HD : (h + 1) * HD]
+    pass_on(2)
     cq_move.wait_recv()
     for h in range(PER):
         r.qs[1, h * TOK : (h + 1) * TOK] = r.q2[1, :, h * HD : (h + 1) * HD]
@@ -370,7 +411,7 @@
     def readouts():
         @pl.when(c > 0)
         def _():
-            tail(0).wait_recv()
+            tail.wait_recv()
 
         b_conv = silu(conv(HD, conv_b))
         r.bconv[...] = b_conv
@@ -382,18 +423,14 @@
             r.mix[h] = exact(read, b_t) * r.within[h]
 
     def project():
-        arrived(h_moves)
-        total = jnp.zeros((TOK, HD), F32)
+        total = jnp.zeros((TOK + 16, HD), F32)
         for j in range(NM):
             total = total + jnp.dot(
-                r.hall[j], wx[j * 512 : (j + 1) * 512], preferred_element_type=F32
+                r.hall[j], r.wx[j * 512 : (j + 1) * 512], preferred_element_type=F32
             )
-        r.ext[8:, :HD] = total.astype(BF16).astype(F32)
-
-        @pl.when(c < LAST)
-        def _():
-            tail(1).start()
-
+        r.ext[:, :HD] = total[8:].astype(BF16).astype(F32)
+
+    def hidden_over_x():
         moves = []
         for d in range(1, NX):
             there = lax.rem(x + d, NX)
@@ -401,17 +438,16 @@
                 at = (d - 1) * 2 + e
                 into = r.hidq.at[e, columns(x, TOK)]
                 moves.append(
-                    go(r.hall.at[2 * there + e], into, r.hq.at[0, at], r.hq.at[1, at], x_peers[d - 1])
+                    go(
+                        r.hall.at[2 * there + e, pl.ds(16, TOK)], into,
+                        r.hq.at[0, at], r.hq.at[1, at], x_peers[d - 1],
+                    )
                 )
         for e in range(2):
-            r.hidq[e, columns(x, TOK)] = r.hall[2 * x + e]
+            r.hidq[e, columns(x, TOK)] = r.hall[2 * x + e, 16:]
         return moves
 
     def states():
-        @pl.when(c > 0)
-        def _():
-            tail(1).wait_recv()
-
         x_pre = conv(0, conv_x)
         x_conv = silu(x_pre)
         r.xpre[...] = x_pre
@@ -480,21 +516,27 @@
 
     receive(1)
     attend(z, True)
+    pass_on(3)
     readouts()
     receive(2)
     attend(right(1), False)
+    pass_on(4)
+    wx_move.wait()
+    project()
+    states()
+    forward = scan(0)
+    next(forward)
+    hq_moves = hidden_over_x()
+    inners()
+    arrived(decay_moves)
+    next(forward)
     attend(left(1), False)
     receive(3)
     attend(right(2), False)
+    next(forward)
     attend(left(2), False)
     receive(4)
-    hq_moves = project()
     attend(right(3), False)
-    states()
-    arrived(decay_moves)
-    forward = scan(0)
-    next(forward)
-    inners()
     next(forward)
     attend(left(3), False)
     attend(right(4), False)
@@ -504,14 +546,12 @@
         go(r.acc.at[1], r.acc_in, r.co.at[0, 0], r.co.at[1, 0], sibling),
         go(r.stat, r.stat_in, r.co.at[0, 1], r.co.at[1, 1], sibling),
     ]
-    next(forward)
     arrived(o_moves)
     other, mine_max = r.stat_in[:, :1], r.m_s[0, :, :1]
     both = jnp.maximum(other, mine_max)
     a0, a1 = jnp.exp2(mine_max - both), jnp.exp2(other - both)
     norm = r.l_s[0, :, :1] * a0 + r.stat_in[:, 64:65] * a1
     r.target[...] = ((r.acc[0] * a0 + r.acc_in[...] * a1) / norm).reshape(PER, TOK, HD)
-    next(forward)
     next(forward)
     for h in range(PER):
         student = r.inner[h] + r.growth[h] * exact(r.read[h], r.inc[0, h])
@@ -536,7 +576,7 @@
     sigma = 1.0 / (1.0 + jnp.exp(-x_pre))
     r.ext2[:TOK] = x_grad * sigma * (1.0 + x_pre * (1.0 - sigma))
     head = remote(
-        r.ext2.at[pl.ds(0, 8)], r.ext2.at[pl.ds(TOK, 8)], r.halo.at[0, 2], r.halo.at[1, 2], previous
+        r.ext2.at[pl.ds(0, 8)], r.ext2.at[pl.ds(TOK, 8)], r.halo.at[0, 1], r.halo.at[1, 1], previous
     )
 
     @pl.when(c > 0)
@@ -585,12 +625,17 @@
 
     @pl.when(c < LAST)
     def _():
-        tail(0).wait_send()
-        tail(1).wait_send()
+        tail.wait_send()
+        end.wait_send()
 
     @pl.when(c > 0)
     def _():
         head.wait_send()
+
+    for way in range(2):
+        for step in range(1, 5):
+            for part in hidden_parts(way, step):
+                hidden_copy(way, step, part).wait_send()
 
     for source, to in FIRST:
 
@@ -627,7 +672,7 @@
             jax.ShapeDtypeStruct((TOK, PER * HD), BF16),
             jax.ShapeDtypeStruct((64, HD), F32),
         ),
-        in_specs=[pl.BlockSpec(memory_space=pltpu.VMEM)] * len(args),
+        in_specs=[pl.BlockSpec(memory_space=pl.ANY if i in (0, 2, 3) else pltpu.VMEM) for i in range(len(args))],
         out_specs=[pl.BlockSpec(memory_space=pltpu.VMEM)] * 2,
         scratch_shapes=list(scratch().values()),
         compiler_params=pltpu.CompilerParams(

time: 111 us -> 110 us (level)
  no operation moved by 1% of the time
where the time goes in v3:
time: 110 us
  Pallas kernels  104 us (95%)
  local copies, waits for them, and re-layouts  4.97 us (5%)
    pallas_call x1, Pallas kernels, local(): pl.pallas_call(layer, out_shape=(jax.ShapeDtypeStruct((TOK, PER * HD), BF...  104 us
    unnamed x22, local copies, waits for them, and re-layouts  4.97 us

profile of v3, /device:TPU:1, one launch (start us, length us, event | category | flops | bytes accessed | tf_op | source)
XLA Modules:
  0.0 109.8 jit_solution(9730214824189358096)
XLA Ops:
  0.6 0.0 copy-start.1
  0.6 0.0 copy-start.8
  0.6 0.9 copy.13
  1.5 0.0 copy-done.8
  1.6 0.0 copy-start.3
  1.6 0.0 copy-start.4
  1.6 0.0 copy-start.5
  1.6 0.0 copy-start.6
  1.6 0.0 copy-start.7
  1.6 0.1 copy.12.step_size
  1.7 0.0 copy-done.1
  1.7 0.5 copy-done.3
  2.3 0.0 copy-done.4
  2.3 0.0 copy-done.5
  2.3 0.0 copy-done.6
  2.3 0.0 copy-done.7
  2.3 0.0 copy-start
  2.3 1.2 %copy-done = bf16[4096,128]{1,0:T(8,128)(2,1)S(1)} copy-done((bf16[4096,128]{1,0:T(8,128)(2,1)S(1)}, bf16[4096,128]{1,0:T(8,128)(2,1)}, u32[]{:S(2)}) %copy-start) | copy-done | bytes 1048600
  3.5 0.0 copy-start.2
  3.5 0.9 copy-done.2
  4.4 104.1 %shard_map.113 = (bf16[128,512]{1,0:T(8,128)(2,1)S(1)}, f32[64,128]{1,0:T(8,128)S(1)}) custom-call(bf16[16,4096]{1,0:T(8,128)(2,1)S(1)} %copy-done.1, bf16[16,2048]{1,0:T(8,128)(2,1)S(1)} %bitcast.4, bf16[128,512]{1,0:T(8,128)(2,1)S(1)} %copy-done.2, bf16[4096,128]{1,0:T(8,128)(2,1)S(1)} %copy-done, f32[128,4]{1,0:T(8,128)S(1)} %copy.12.step_size, ...), custom_call_target="tpu_custom_call" | custom-call | tf_op jit(solution)/shard_map/pallas_call | solution.py:669
  108.6 0.7 copy.16
  109.2 0.6 copy.17
Async XLA Ops:
  0.6 1.1 %copy-start.1 = (bf16[16,4096]{1,0:T(8,128)(2,1)S(1)}, bf16[16,4096]{1,0:T(8,128)(2,1)}, u32[]{:S(2)}) copy-start(bf16[16,4096]{1,0:T(8,128)(2,1)} %q_in.1) | copy-start | bytes 393220
  0.6 0.9 copy-start.8
  1.6 0.7 copy-start.3
  1.6 0.7 copy-start.4
  1.6 0.7 copy-start.5
  1.6 0.7 copy-start.6
  1.6 0.7 copy-start.7
  2.3 1.2 %copy-start = (bf16[4096,128]{1,0:T(8,128)(2,1)S(1)}, bf16[4096,128]{1,0:T(8,128)(2,1)}, u32[]{:S(2)}) copy-start(bf16[4096,128]{1,0:T(8,128)(2,1)} %wx.1) | copy-start | bytes 3145732
  3.5 0.9 copy-start.2

commit v4 on v3

--- a/solution.py
+++ b/solution.py
@@ -68,13 +68,14 @@
         "hall": vm((NM, TOK + 16, 512), BF16),
         "wx": vm((4096, HD), BF16),
         "hidq": vm((2, NX * TOK, 512), BF16),
-        "qs": vm((2, PER * TOK, HD), BF16),
-        "m_s": vm((2, PER * TOK, HD), F32),
-        "l_s": vm((2, PER * TOK, HD), F32),
-        "acc": vm((2, PER * TOK, HD), F32),
-        "stat": vm((PER * TOK, HD), F32),
-        "acc_in": vm((PER * TOK, HD), F32),
-        "stat_in": vm((PER * TOK, HD), F32),
+        "qs": vm((2 * PER * TOK, HD), BF16),
+        "m_s": vm((8, 2 * PER * TOK), F32),
+        "l_s": vm((8, 2 * PER * TOK), F32),
+        "acc": vm((HD, 2 * PER * TOK), F32),
+        "stat": vm((8, PER * TOK), F32),
+        "acc_in": vm((HD, PER * TOK), F32),
+        "stat_in": vm((8, PER * TOK), F32),
+        "hid_t": vm((2, 512, NX * TOK), BF16),
         "target": vm((PER, TOK, HD), F32),
         "ext": vm((TOK + 8, 6 * HD), F32),
         "ext2": vm((TOK + 8, HD), F32),
@@ -164,10 +165,6 @@
     def columns(i, width):
         return pl.ds(pl.multiple_of(i * width, width), width)
 
-    kv_moves = [
-        go(kv_in.at[:, columns(p[3], 256)], r.kvb.at[z, x, rows], r.ykv.at[0, d], r.ykv.at[1, d], p)
-        for d, p in enumerate(y_peers)
-    ]
     def hidden_copy(way, step, part):
         block = lax.rem(m - (step - 1) + NM, NM) if way == 0 else lax.rem(m + step - 1, NM)
         peer = y_peers[0] if way == 0 else y_peers[-1]
@@ -198,6 +195,10 @@
     for part in range(2):
         for way in range(2):
             hidden_copy(way, 1, part).start()
+    kv_moves = [
+        go(kv_in.at[:, columns(p[3], 256)], r.kvb.at[z, x, rows], r.ykv.at[0, d], r.ykv.at[1, d], p)
+        for d, p in enumerate(y_peers)
+    ]
     q_moves = [
         go(q_in.at[:, columns(p[3], 512)], r.q2.at[0, rows], r.yq.at[0, d], r.yq.at[1, d], p)
         for d, p in enumerate(y_peers)
@@ -333,11 +334,11 @@
     r.drecv[chip] = r.dsend[lax.div(x, 2)]
 
     for h in range(PER):
-        r.qs[0, h * TOK : (h + 1) * TOK] = r.q2[0, :, h * HD : (h + 1) * HD]
+        r.qs[h * TOK : (h + 1) * TOK] = r.q2[0, :, h * HD : (h + 1) * HD]
     pass_on(2)
     cq_move.wait_recv()
     for h in range(PER):
-        r.qs[1, h * TOK : (h + 1) * TOK] = r.q2[1, :, h * HD : (h + 1) * HD]
+        r.qs[(PER + h) * TOK : (PER + h + 1) * TOK] = r.q2[1, :, h * HD : (h + 1) * HD]
 
     def attend(column, masked):
         for xs in range(NX - 1):
@@ -346,36 +347,36 @@
             def _(xs=xs):
                 across(column, xs).wait_recv()
 
-        def tile(i, carry):
-            side, first = lax.div(i, 2), pl.multiple_of(lax.rem(i, 2) * 256, 256)
-            at = pl.ds(first, 256)
-            block = r.kvb[column].reshape(NX * TOK, 2 * HD)
-            s = lax.dot_general(
-                r.qs[side, at], block[:, :HD], (((1,), (1,)), ((), ())), preferred_element_type=F32
-            )
-            if masked:
-                key = lax.broadcasted_iota(jnp.int32, (256, NX * TOK), 1)
-                query = lax.broadcasted_iota(jnp.int32, (256, NX * TOK), 0)
-                core = jnp.where(side == 0, k, 1 - k)
-                ahead = (key - x * TOK) + k * TOK - (lax.rem(query, TOK) + core * TOK)
-                allowed = (key < x * TOK) | ((ahead <= 0) & (key < (x + 1) * TOK))
-                s = jnp.where(allowed, s * SCALE2, NEG)
-            else:
-                key = lax.broadcasted_iota(jnp.int32, (1, NX * TOK), 1)
-                limit = jnp.where(column < z, (x + 1) * TOK, x * TOK)
-                s = s * SCALE2 + jnp.where(key < limit, 0.0, NEG)
-            before = r.m_s[side, at, :1]
-            now = jnp.maximum(before, jnp.max(s, axis=1, keepdims=True))
-            p = jnp.exp2(s - now)
-            alpha = jnp.exp2(before - now)
-            r.m_s[side, at] = jnp.broadcast_to(now, (256, HD))
-            r.l_s[side, at] = r.l_s[side, at] * alpha + jnp.sum(p, axis=1, keepdims=True)
-            r.acc[side, at] = r.acc[side, at] * alpha + jnp.dot(
-                p.astype(BF16), block[:, HD:], preferred_element_type=F32
-            )
-            return carry
-
-        lax.fori_loop(0, 4, tile, 0)
+        block = r.kvb[column].reshape(NX * TOK, 2 * HD)
+        scores = lax.dot_general(
+            block[:, :HD], r.qs[...], (((1,), (1,)), ((), ())), preferred_element_type=F32
+        )
+        parts = [scores[b * TOK : (b + 1) * TOK] for b in range(NX)]
+        if masked:
+            key = lax.broadcasted_iota(jnp.int32, (TOK, 2 * PER * TOK), 0)
+            query = lax.broadcasted_iota(jnp.int32, (TOK, 2 * PER * TOK), 1)
+            core = jnp.where(query < PER * TOK, k, 1 - k)
+            own = key + k * TOK <= lax.rem(query, TOK) + core * TOK
+            parts = [jnp.where((b != x) | own, part, NEG) for b, part in enumerate(parts)]
+            shut = [jnp.where(b <= x, 0.0, NEG) for b in range(NX)]
+        else:
+            shut = [jnp.where((b < x) | ((b == x) & (column < z)), 0.0, NEG) for b in range(NX)]
+        before = now = r.m_s[:1]
+        for part, off in zip(parts, shut, strict=True):
+            now = jnp.maximum(now, jnp.max(part, axis=0, keepdims=True) * SCALE2 + off)
+        alpha = jnp.exp2(before - now)
+        parts = [
+            jnp.exp2(part * SCALE2 - (now - off)) for part, off in zip(parts, shut, strict=True)
+        ]
+        total = r.l_s[:1] * alpha
+        for part in parts:
+            total = total + jnp.sum(part, axis=0, keepdims=True)
+        r.l_s[:1] = total
+        r.m_s[:1] = now
+        weights = jnp.concatenate([part.astype(BF16) for part in parts], axis=0)
+        r.acc[...] = r.acc[...] * alpha + lax.dot_general(
+            block[:, HD:], weights, (((0,), (0,)), ((), ())), preferred_element_type=F32
+        )
 
     def receive(step):
         for way in range(2):
@@ -516,42 +517,46 @@
 
     receive(1)
     attend(z, True)
+    readouts()
     pass_on(3)
-    readouts()
     receive(2)
     attend(right(1), False)
+    attend(left(1), False)
     pass_on(4)
     wx_move.wait()
     project()
     states()
     forward = scan(0)
     next(forward)
-    hq_moves = hidden_over_x()
+    receive(3)
     inners()
     arrived(decay_moves)
     next(forward)
-    attend(left(1), False)
-    receive(3)
     attend(right(2), False)
-    next(forward)
     attend(left(2), False)
     receive(4)
+    hq_moves = hidden_over_x()
     attend(right(3), False)
+    attend(left(3), False)
     next(forward)
-    attend(left(3), False)
     attend(right(4), False)
-    lane = lax.broadcasted_iota(jnp.int32, (PER * TOK, HD), 1)
-    r.stat[...] = jnp.where(lane < 64, r.m_s[1], r.l_s[1])
+    half = PER * TOK
+    r.stat[:1] = r.m_s[:1, half:]
+    r.stat[1:2] = r.l_s[:1, half:]
+    r.stat[2:] = jnp.zeros((6, half), F32)
     o_moves = [
-        go(r.acc.at[1], r.acc_in, r.co.at[0, 0], r.co.at[1, 0], sibling),
+        go(r.acc.at[:, pl.ds(half, half)], r.acc_in, r.co.at[0, 0], r.co.at[1, 0], sibling),
         go(r.stat, r.stat_in, r.co.at[0, 1], r.co.at[1, 1], sibling),
     ]
+    next(forward)
     arrived(o_moves)
-    other, mine_max = r.stat_in[:, :1], r.m_s[0, :, :1]
+    other, mine_max = r.stat_in[:1], r.m_s[:1, :half]
     both = jnp.maximum(other, mine_max)
     a0, a1 = jnp.exp2(mine_max - both), jnp.exp2(other - both)
-    norm = r.l_s[0, :, :1] * a0 + r.stat_in[:, 64:65] * a1
-    r.target[...] = ((r.acc[0] * a0 + r.acc_in[...] * a1) / norm).reshape(PER, TOK, HD)
+    norm = r.l_s[:1, :half] * a0 + r.stat_in[1:2] * a1
+    result = (r.acc[:, :half] * a0 + r.acc_in[...] * a1) / norm
+    for h in range(PER):
+        r.target[h] = result[:, h * TOK : (h + 1) * TOK].T
     next(forward)
     for h in range(PER):
         student = r.inner[h] + r.growth[h] * exact(r.read[h], r.inc[0, h])
@@ -567,6 +572,9 @@
         up = r.up[h]
         x_grad = x_grad + step_of(h) * exact(r.mix[h].T, up) + skip_gain[:, h : h + 1] * up
     next(backward)
+    arrived(hq_moves)
+    for e in range(2):
+        r.hid_t[e] = r.hidq[e].T
     next(backward)
     next(backward)
     b_conv = r.bconv[...]
@@ -599,12 +607,9 @@
     moves = [
         go(here, here, r.igs.at[0, d], r.igs.at[1, d], p) for d, p in enumerate(x_peers)
     ]
-    arrived(hq_moves)
     arrived(moves)
     for e in range(2):
-        product = lax.dot_general(
-            r.hidq[e], r.ig[...], (((0,), (0,)), ((), ())), preferred_element_type=F32
-        )
+        product = jnp.dot(r.hid_t[e], r.ig[...], preferred_element_type=F32)
         r.part[4 * e : 4 * e + 4] = product.reshape(4, NK, 64, HD)
     go(r.part.at[:, 1 - k], r.wrecv, r.wc.at[0], r.wc.at[1], sibling).wait_recv()
     for i in range(NZ):

time: 110 us -> 107 us (0.973)
  Pallas kernels: 104 us -> 101 us
    pallas_call x1, Pallas kernels: 104 us -> 101 us  [local(): pl.pallas_call(layer, out_shape=(jax.ShapeDtypeStruct((TOK, PER * HD), BF...]
where the time goes in v4:
time: 107 us
  Pallas kernels  101 us (94%)
  local copies, waits for them, and re-layouts  4.97 us (5%)
    pallas_call x1, Pallas kernels, local(): pl.pallas_call(layer, out_shape=(jax.ShapeDtypeStruct((TOK, PER * HD), BF...  101 us
    unnamed x22, local copies, waits for them, and re-layouts  4.97 us

profile of v4, /device:TPU:1, one launch (start us, length us, event | category | flops | bytes accessed | tf_op | source)
XLA Modules:
  0.0 107.1 jit_solution(15255888714475610668)
XLA Ops:
  0.6 0.0 copy-start.1
  0.6 0.0 copy-start.8
  0.6 0.9 copy.13
  1.5 0.0 copy-done.8
  1.6 0.0 copy-start.3
  1.6 0.0 copy-start.4
  1.6 0.0 copy-start.5
  1.6 0.0 copy-start.6
  1.6 0.0 copy-start.7
  1.6 0.1 copy.12.step_size
  1.7 0.0 copy-done.1
  1.7 0.5 copy-done.3
  2.3 0.0 copy-done.4
  2.3 0.0 copy-done.5
  2.3 0.0 copy-done.6
  2.3 0.0 copy-done.7
  2.3 0.0 copy-start
  2.3 1.2 %copy-done = bf16[4096,128]{1,0:T(8,128)(2,1)S(1)} copy-done((bf16[4096,128]{1,0:T(8,128)(2,1)S(1)}, bf16[4096,128]{1,0:T(8,128)(2,1)}, u32[]{:S(2)}) %copy-start) | copy-done | bytes 1048600
  3.5 0.0 copy-start.2
  3.5 0.9 copy-done.2
  4.4 101.4 %shard_map.113 = (bf16[128,512]{1,0:T(8,128)(2,1)S(1)}, f32[64,128]{1,0:T(8,128)S(1)}) custom-call(bf16[16,4096]{1,0:T(8,128)(2,1)S(1)} %copy-done.1, bf16[16,2048]{1,0:T(8,128)(2,1)S(1)} %bitcast.4, bf16[128,512]{1,0:T(8,128)(2,1)S(1)} %copy-done.2, bf16[4096,128]{1,0:T(8,128)(2,1)S(1)} %copy-done, f32[128,4]{1,0:T(8,128)S(1)} %copy.12.step_size, ...), custom_call_target="tpu_custom_call" | custom-call | tf_op jit(solution)/shard_map/pallas_call | solution.py:674
  105.9 0.7 copy.16
  106.5 0.6 copy.17
Async XLA Ops:
  0.6 1.1 %copy-start.1 = (bf16[16,4096]{1,0:T(8,128)(2,1)S(1)}, bf16[16,4096]{1,0:T(8,128)(2,1)}, u32[]{:S(2)}) copy-start(bf16[16,4096]{1,0:T(8,128)(2,1)} %q_in.1) | copy-start | bytes 393220
  0.6 0.9 copy-start.8
  1.6 0.7 copy-start.3
  1.6 0.7 copy-start.4
  1.6 0.7 copy-start.5
  1.6 0.7 copy-start.6
  1.6 0.7 copy-start.7
  2.3 1.2 %copy-start = (bf16[4096,128]{1,0:T(8,128)(2,1)S(1)}, bf16[4096,128]{1,0:T(8,128)(2,1)}, u32[]{:S(2)}) copy-start(bf16[4096,128]{1,0:T(8,128)(2,1)} %wx.1) | copy-start | bytes 3145732
  3.5 0.9 copy-start.2

commit v5 on v4

--- a/solution.py
+++ b/solution.py
@@ -379,21 +379,19 @@
         )
 
     def receive(step):
-        for way in range(2):
-            if way == 1 and step == 4:
-                continue
-            column = lax.rem(z - step + NZ, NZ) if way == 0 else lax.rem(z + step, NZ)
-            for xs in range(NX):
-
-                @pl.when(in_ring(xs))
-                def _(way=way, xs=xs):
-                    ring_copy(way, step, xs).wait_recv()
-                    if step < (4, 3)[way]:
-                        ring_copy(way, step + 1, xs).start()
-                    if xs < 3:
-
-                        @pl.when(x == xs)
-                        def _():
+        for own in (True, False):
+            for xs in range(NX) if own else range(NX - 2):
+
+                @pl.when((x == xs) if own else in_ring(xs) & (x != xs))
+                def _(own=own, xs=xs):
+                    for way in range(2):
+                        if way == 1 and step == 4:
+                            continue
+                        column = right(step) if way == 0 else left(step)
+                        ring_copy(way, step, xs).wait_recv()
+                        if step < (4, 3)[way]:
+                            ring_copy(way, step + 1, xs).start()
+                        if own and xs < 3:
                             across(column, xs).start()
 
     def right(step):
@@ -409,15 +407,16 @@
             total = total + taps[j : j + 1, :] * r.ext[5 + j : 5 + j + TOK, first : first + width]
         return total
 
-    def readouts():
+    def inputs():
         @pl.when(c > 0)
         def _():
             tail.wait_recv()
 
-        b_conv = silu(conv(HD, conv_b))
-        r.bconv[...] = b_conv
+        r.bconv[...] = silu(conv(HD, conv_b))
+
+    def readouts():
         c_conv = silu(conv(2 * HD, conv_c))
-        b_t = b_conv.T
+        b_t = r.bconv[...].T
         for h in range(PER):
             read = c_conv[:, h * HD : (h + 1) * HD]
             r.read[h] = read
@@ -516,29 +515,30 @@
         yield
 
     receive(1)
-    attend(z, True)
-    readouts()
     pass_on(3)
     receive(2)
-    attend(right(1), False)
-    attend(left(1), False)
+    inputs()
+    wx_move.wait()
     pass_on(4)
-    wx_move.wait()
     project()
     states()
     forward = scan(0)
     next(forward)
+    arrived(decay_moves)
     receive(3)
+    next(forward)
+    hq_moves = hidden_over_x()
+    attend(z, True)
+    attend(right(1), False)
+    attend(left(1), False)
+    receive(4)
+    readouts()
     inners()
-    arrived(decay_moves)
+    attend(right(2), False)
     next(forward)
-    attend(right(2), False)
     attend(left(2), False)
-    receive(4)
-    hq_moves = hidden_over_x()
     attend(right(3), False)
     attend(left(3), False)
-    next(forward)
     attend(right(4), False)
     half = PER * TOK
     r.stat[:1] = r.m_s[:1, half:]
@@ -571,10 +571,46 @@
     for h in range(PER):
         up = r.up[h]
         x_grad = x_grad + step_of(h) * exact(r.mix[h].T, up) + skip_gain[:, h : h + 1] * up
-    next(backward)
     arrived(hq_moves)
     for e in range(2):
         r.hid_t[e] = r.hidq[e].T
+    next(backward)
+
+    for move in sent:
+        move.wait_send()
+    sent.clear()
+
+    @pl.when(c < LAST)
+    def _():
+        tail.wait_send()
+        end.wait_send()
+
+    for way in range(2):
+        for step in range(1, 5):
+            for part in hidden_parts(way, step):
+                hidden_copy(way, step, part).wait_send()
+
+    for source, to in FIRST:
+
+        @pl.when(x == source)
+        def _(source=source, to=to):
+            first_copy(source, to).wait_send()
+
+    for xs in range(NX):
+
+        @pl.when(in_ring(xs))
+        def _(xs=xs):
+            for way in range(2):
+                for step in range(1, (4, 3)[way] + 1):
+                    ring_copy(way, step, xs).wait_send()
+
+        if xs < 3:
+
+            @pl.when(x == xs)
+            def _(xs=xs):
+                for column in range(NZ):
+                    across(column, xs).wait_send()
+
     next(backward)
     next(backward)
     b_conv = r.bconv[...]
@@ -628,40 +664,9 @@
     for move in sent:
         move.wait_send()
 
-    @pl.when(c < LAST)
-    def _():
-        tail.wait_send()
-        end.wait_send()
-
     @pl.when(c > 0)
     def _():
         head.wait_send()
-
-    for way in range(2):
-        for step in range(1, 5):
-            for part in hidden_parts(way, step):
-                hidden_copy(way, step, part).wait_send()
-
-    for source, to in FIRST:
-
-        @pl.when(x == source)
-        def _(source=source, to=to):
-            first_copy(source, to).wait_send()
-
-    for xs in range(NX):
-
-        @pl.when(in_ring(xs))
-        def _(xs=xs):
-            for way in range(2):
-                for step in range(1, (4, 3)[way] + 1):
-                    ring_copy(way, step, xs).wait_send()
-
-        if xs < 3:
-
-            @pl.when(x == xs)
-            def _(xs=xs):
-                for column in range(NZ):
-                    across(column, xs).wait_send()
 
 
 def local(

time: 107 us -> 105 us (0.981)
  Pallas kernels: 101 us -> 99.5 us
    pallas_call x1, Pallas kernels: 101 us -> 99.5 us  [local(): pl.pallas_call(layer, out_shape=(jax.ShapeDtypeStruct((TOK, PER * HD), BF...]
where the time goes in v5:
time: 105 us
  Pallas kernels  99.5 us (95%)
  local copies, waits for them, and re-layouts  4.97 us (5%)
    pallas_call x1, Pallas kernels, local(): pl.pallas_call(layer, out_shape=(jax.ShapeDtypeStruct((TOK, PER * HD), BF...  99.5 us
    unnamed x22, local copies, waits for them, and re-layouts  4.97 us

profile of v5, /device:TPU:1, one launch (start us, length us, event | category | flops | bytes accessed | tf_op | source)
XLA Modules:
  0.0 105.2 jit_solution(12899991300370708042)
XLA Ops:
  0.6 0.0 copy-start.1
  0.6 0.0 copy-start.8
  0.6 0.9 copy.13
  1.5 0.0 copy-done.8
  1.6 0.0 copy-start.3
  1.6 0.0 copy-start.4
  1.6 0.0 copy-start.5
  1.6 0.0 copy-start.6
  1.6 0.0 copy-start.7
  1.6 0.1 copy.12.step_size
  1.7 0.0 copy-done.1
  1.7 0.5 copy-done.3
  2.3 0.0 copy-done.4
  2.3 0.0 copy-done.5
  2.3 0.0 copy-done.6
  2.3 0.0 copy-done.7
  2.3 0.0 copy-start
  2.3 1.2 %copy-done = bf16[4096,128]{1,0:T(8,128)(2,1)S(1)} copy-done((bf16[4096,128]{1,0:T(8,128)(2,1)S(1)}, bf16[4096,128]{1,0:T(8,128)(2,1)}, u32[]{:S(2)}) %copy-start) | copy-done | bytes 1048600
  3.5 0.0 copy-start.2
  3.5 0.9 copy-done.2
  4.4 99.5 %shard_map.113 = (bf16[128,512]{1,0:T(8,128)(2,1)S(1)}, f32[64,128]{1,0:T(8,128)S(1)}) custom-call(bf16[16,4096]{1,0:T(8,128)(2,1)S(1)} %copy-done.1, bf16[16,2048]{1,0:T(8,128)(2,1)S(1)} %bitcast.4, bf16[128,512]{1,0:T(8,128)(2,1)S(1)} %copy-done.2, bf16[4096,128]{1,0:T(8,128)(2,1)S(1)} %copy-done, f32[128,4]{1,0:T(8,128)S(1)} %copy.12.step_size, ...), custom_call_target="tpu_custom_call" | custom-call | tf_op jit(solution)/shard_map/pallas_call | solution.py:679
  103.9 0.7 copy.16
  104.6 0.6 copy.17
Async XLA Ops:
  0.6 1.1 %copy-start.1 = (bf16[16,4096]{1,0:T(8,128)(2,1)S(1)}, bf16[16,4096]{1,0:T(8,128)(2,1)}, u32[]{:S(2)}) copy-start(bf16[16,4096]{1,0:T(8,128)(2,1)} %q_in.1) | copy-start | bytes 393220
  0.6 0.9 copy-start.8
  1.6 0.7 copy-start.3
  1.6 0.7 copy-start.4
  1.6 0.7 copy-start.5
  1.6 0.7 copy-start.6
  1.6 0.7 copy-start.7
  2.3 1.2 %copy-start = (bf16[4096,128]{1,0:T(8,128)(2,1)S(1)}, bf16[4096,128]{1,0:T(8,128)(2,1)}, u32[]{:S(2)}) copy-start(bf16[4096,128]{1,0:T(8,128)(2,1)} %wx.1) | copy-start | bytes 3145732
  3.5 0.9 copy-start.2

commit v6 on v5

--- a/solution.py
+++ b/solution.py
@@ -79,6 +79,10 @@
         "target": vm((PER, TOK, HD), F32),
         "ext": vm((TOK + 8, 6 * HD), F32),
         "ext2": vm((TOK + 8, HD), F32),
+        "ext3": vm((24, HD), F32),
+        "last": vm((NX, 16, HD), F32),
+        "share": vm((16, HD), F32),
+        "shares": vm((NX, 16, HD), F32),
         "growth": vm((PER, TOK, TOK), F32),
         "to_end": vm((PER, TOK, TOK), F32),
         "within": vm((PER, TOK, TOK), F32),
@@ -123,7 +127,8 @@
         "zs": dma(2, 62),
         "bs": dma(2, 62),
         "ks": dma(2, 2),
-        "igs": dma(2, 3),
+        "igs": dma(2, 6),
+        "hs": dma(2, NX),
         "wc": dma(2),
         "wz": dma(2, 7),
     }
@@ -147,7 +152,9 @@
         return (lax.div(i, NZ * NK), lax.rem(lax.div(i, NK), NZ), lax.rem(i, NK), m)
 
     following, previous = at_ctx(lax.rem(c + 1, LAST + 1)), at_ctx(lax.rem(c + LAST, LAST + 1))
-    greet([*y_peers, *plane, sibling, following, previous])
+    before = [(lax.rem(previous[0] + i, NX), *previous[1:]) for i in range(NX)]
+    after = [(lax.rem(following[0] + i, NX), *following[1:]) for i in range(NX)]
+    greet([*y_peers, *plane, sibling, *before, *after])
     sent = []
 
     def go(*args):
@@ -197,10 +204,6 @@
             hidden_copy(way, 1, part).start()
     kv_moves = [
         go(kv_in.at[:, columns(p[3], 256)], r.kvb.at[z, x, rows], r.ykv.at[0, d], r.ykv.at[1, d], p)
-        for d, p in enumerate(y_peers)
-    ]
-    q_moves = [
-        go(q_in.at[:, columns(p[3], 512)], r.q2.at[0, rows], r.yq.at[0, d], r.yq.at[1, d], p)
         for d, p in enumerate(y_peers)
     ]
     mine = [
@@ -296,8 +299,34 @@
         hidden_copy(way, 1, 2).start()
     pass_on(1)
 
-    arrived(q_moves)
-    cq_move = go(r.q2.at[0], r.q2.at[1], r.cq.at[0], r.cq.at[1], sibling)
+    q_moves = [
+        go(q_in.at[:, columns(p[3], 512)], r.q2.at[0, rows], r.yq.at[0, d], r.yq.at[1, d], p)
+        for d, p in enumerate(y_peers)
+    ]
+    def tail(i):
+        at = (pl.ds(HD, HD), pl.ds(2 * HD, 4 * HD))[i]
+        return remote(
+            r.ext.at[pl.ds(TOK, 8), at], r.ext.at[pl.ds(0, 8), at],
+            r.halo.at[0, i], r.halo.at[1, i], following,
+        )
+
+    def pass_tail(i):
+        @pl.when(c < LAST)
+        def _():
+            tail(i).start()
+
+    def tail_here(i):
+        @pl.when(c > 0)
+        def _():
+            tail(i).wait_recv()
+
+    r.ext[8:, HD : 2 * HD] = r.kvb[z, x, :, :HD].astype(F32)
+    pass_tail(0)
+
+    @pl.when(c == 0)
+    def _():
+        r.ext[:8, HD:] = jnp.zeros((8, 5 * HD), F32)
+
     for source, to in FIRST:
 
         @pl.when(x == to)
@@ -306,39 +335,21 @@
             ring_copy(0, 1, source).start()
             ring_copy(1, 1, source).start()
 
-    r.ext[8:, HD : 2 * HD] = r.kvb[z, x, :, :HD].astype(F32)
-    r.ext[8:, 2 * HD :] = r.q2[0].astype(F32)
-
-    at = pl.ds(HD, 5 * HD)
-    tail = remote(
-        r.ext.at[pl.ds(TOK, 8), at], r.ext.at[pl.ds(0, 8), at], r.halo.at[0, 0], r.halo.at[1, 0], following
-    )
-
-    @pl.when(c < LAST)
-    def _():
-        tail.start()
-
-    @pl.when(c == 0)
-    def _():
-        r.ext[:8, HD:] = jnp.zeros((8, 5 * HD), F32)
-
-    d_move.wait_recv()
-    for h in range(2):
-        chip_decay = r.dec[...] * r.dsib[...]
-        decay_row = jnp.where(k == 0, chip_decay[h : h + 1], chip_decay[2 + h : 3 + h])
-        r.dsend[h] = jnp.broadcast_to(decay_row, (8, HD))
-    decay_moves = [
-        go(r.dsend.at[lax.div(p[0], 2)], r.drecv.at[chip], r.ds.at[0, i], r.ds.at[1, i], p)
-        for i, p in enumerate(plane)
-    ]
-    r.drecv[chip] = r.dsend[lax.div(x, 2)]
-
-    for h in range(PER):
-        r.qs[h * TOK : (h + 1) * TOK] = r.q2[0, :, h * HD : (h + 1) * HD]
     pass_on(2)
-    cq_move.wait_recv()
-    for h in range(PER):
-        r.qs[(PER + h) * TOK : (PER + h + 1) * TOK] = r.q2[1, :, h * HD : (h + 1) * HD]
+
+    def queries():
+        arrived(q_moves)
+        move = go(r.q2.at[0], r.q2.at[1], r.cq.at[0], r.cq.at[1], sibling)
+        r.ext[8:, 2 * HD :] = r.q2[0].astype(F32)
+        pass_tail(1)
+        for h in range(PER):
+            r.qs[h * TOK : (h + 1) * TOK] = r.q2[0, :, h * HD : (h + 1) * HD]
+        return move
+
+    def sibling_queries(move):
+        move.wait_recv()
+        for h in range(PER):
+            r.qs[(PER + h) * TOK : (PER + h + 1) * TOK] = r.q2[1, :, h * HD : (h + 1) * HD]
 
     def attend(column, masked):
         for xs in range(NX - 1):
@@ -408,13 +419,11 @@
         return total
 
     def inputs():
-        @pl.when(c > 0)
-        def _():
-            tail.wait_recv()
-
+        tail_here(0)
         r.bconv[...] = silu(conv(HD, conv_b))
 
     def readouts():
+        tail_here(1)
         c_conv = silu(conv(2 * HD, conv_c))
         b_t = r.bconv[...].T
         for h in range(PER):
@@ -516,6 +525,17 @@
 
     receive(1)
     pass_on(3)
+    d_move.wait_recv()
+    for h in range(2):
+        chip_decay = r.dec[...] * r.dsib[...]
+        decay_row = jnp.where(k == 0, chip_decay[h : h + 1], chip_decay[2 + h : 3 + h])
+        r.dsend[h] = jnp.broadcast_to(decay_row, (8, HD))
+    decay_moves = [
+        go(r.dsend.at[lax.div(p[0], 2)], r.drecv.at[chip], r.ds.at[0, i], r.ds.at[1, i], p)
+        for i, p in enumerate(plane)
+    ]
+    r.drecv[chip] = r.dsend[lax.div(x, 2)]
+
     receive(2)
     inputs()
     wx_move.wait()
@@ -524,10 +544,12 @@
     states()
     forward = scan(0)
     next(forward)
-    arrived(decay_moves)
+    cq_move = queries()
     receive(3)
     next(forward)
+    arrived(decay_moves)
     hq_moves = hidden_over_x()
+    sibling_queries(cq_move)
     attend(z, True)
     attend(right(1), False)
     attend(left(1), False)
@@ -582,7 +604,8 @@
 
     @pl.when(c < LAST)
     def _():
-        tail.wait_send()
+        tail(0).wait_send()
+        tail(1).wait_send()
         end.wait_send()
 
     for way in range(2):
@@ -619,31 +642,48 @@
     x_pre = r.xpre[...]
     sigma = 1.0 / (1.0 + jnp.exp(-x_pre))
     r.ext2[:TOK] = x_grad * sigma * (1.0 + x_pre * (1.0 - sigma))
-    head = remote(
-        r.ext2.at[pl.ds(0, 8)], r.ext2.at[pl.ds(TOK, 8)], r.halo.at[0, 1], r.halo.at[1, 1], previous
-    )
+    r.ext2[TOK:] = jnp.zeros((8, HD), F32)
+    r.ext3[:16] = jnp.zeros((16, HD), F32)
+    r.ext3[16:] = r.ext2[:8]
+    grad, share = jnp.zeros((TOK, HD), F32), jnp.zeros((16, HD), F32)
+    for j in range(CONV):
+        first = CONV - 1 - j
+        grad = grad + conv_x[j : j + 1, :] * r.ext2[first : first + TOK]
+        share = share + conv_x[j : j + 1, :] * r.ext3[first : first + 16]
+    r.share[...] = share
+    r.last[x] = grad[TOK - 16 :]
+
+    def share_copy(i):
+        return remote(
+            r.share, r.shares.at[previous[0]], r.hs.at[0, i], r.hs.at[1, previous[0]], before[i]
+        )
 
     @pl.when(c > 0)
     def _():
-        head.start()
-
-    @pl.when(c == LAST)
-    def _():
-        r.ext2[TOK:] = jnp.zeros((8, HD), F32)
-
-    @pl.when(c < LAST)
-    def _():
-        head.wait_recv()
-
-    grad = jnp.zeros((TOK, HD), F32)
-    for j in range(CONV):
-        grad = grad + conv_x[j : j + 1, :] * r.ext2[CONV - 1 - j : CONV - 1 - j + TOK]
-    here = r.ig.at[columns(x, TOK)]
-    here[...] = grad.astype(BF16)
-    moves = [
-        go(here, here, r.igs.at[0, d], r.igs.at[1, d], p) for d, p in enumerate(x_peers)
-    ]
+        for i in range(NX):
+            share_copy(i).start()
+
+    here = r.ig.at[pl.ds(pl.multiple_of(x * TOK, TOK), TOK - 16)]
+    here[...] = grad[: TOK - 16].astype(BF16)
+    moves = []
+    for d, p in enumerate(x_peers):
+        moves.append(go(r.last.at[x], r.last.at[x], r.igs.at[0, d], r.igs.at[1, d], p))
+        moves.append(go(here, here, r.igs.at[0, 3 + d], r.igs.at[1, 3 + d], p))
+    at_end = (z == NZ - 1) & (k == NK - 1)
+    for i in range(NX):
+        arrival = remote(r.share, r.shares.at[i], r.hs.at[0, i], r.hs.at[1, i], sibling)
+        if i < NX - 1:
+            arrival.wait_recv()
+        else:
+            pl.when(jnp.logical_not(at_end))(arrival.wait_recv)
+
+            @pl.when(at_end)
+            def _(i=i):
+                r.shares[i] = jnp.zeros((16, HD), F32)
+
     arrived(moves)
+    for i in range(NX):
+        r.ig[(i + 1) * TOK - 16 : (i + 1) * TOK] = (r.last[i] + r.shares[i]).astype(BF16)
     for e in range(2):
         product = jnp.dot(r.hid_t[e], r.ig[...], preferred_element_type=F32)
         r.part[4 * e : 4 * e + 4] = product.reshape(4, NK, 64, HD)
@@ -666,7 +706,8 @@
 
     @pl.when(c > 0)
     def _():
-        head.wait_send()
+        for i in range(NX):
+            share_copy(i).wait_send()
 
 
 def local(

time: 105 us -> 102 us (0.971)
  Pallas kernels: 99.5 us -> 96.5 us
    pallas_call x1, Pallas kernels: 99.5 us -> 96.5 us  [local(): pl.pallas_call(layer, out_shape=(jax.ShapeDtypeStruct((TOK, PER * HD), BF...]
where the time goes in v6:
time: 102 us
  Pallas kernels  96.5 us (95%)
  local copies, waits for them, and re-layouts  4.97 us (5%)
    pallas_call x1, Pallas kernels, local(): pl.pallas_call(layer, out_shape=(jax.ShapeDtypeStruct((TOK, PER * HD), BF...  96.5 us
    unnamed x22, local copies, waits for them, and re-layouts  4.97 us

profile of v6, /device:TPU:1, one launch (start us, length us, event | category | flops | bytes accessed | tf_op | source)
XLA Modules:
  0.0 102.2 jit_solution(8396421222997389048)
XLA Ops:
  0.6 0.0 copy-start.1
  0.6 0.0 copy-start.8
  0.6 0.9 copy.13
  1.5 0.0 copy-done.8
  1.6 0.0 copy-start.3
  1.6 0.0 copy-start.4
  1.6 0.0 copy-start.5
  1.6 0.0 copy-start.6
  1.6 0.0 copy-start.7
  1.6 0.1 copy.12.step_size
  1.7 0.0 copy-done.1
  1.7 0.5 copy-done.3
  2.3 0.0 copy-done.4
  2.3 0.0 copy-done.5
  2.3 0.0 copy-done.6
  2.3 0.0 copy-done.7
  2.3 0.0 copy-start
  2.3 1.2 %copy-done = bf16[4096,128]{1,0:T(8,128)(2,1)S(1)} copy-done((bf16[4096,128]{1,0:T(8,128)(2,1)S(1)}, bf16[4096,128]{1,0:T(8,128)(2,1)}, u32[]{:S(2)}) %copy-start) | copy-done | bytes 1048600
  3.5 0.0 copy-start.2
  3.5 0.9 copy-done.2
  4.4 96.5 %shard_map.113 = (bf16[128,512]{1,0:T(8,128)(2,1)S(1)}, f32[64,128]{1,0:T(8,128)S(1)}) custom-call(bf16[16,4096]{1,0:T(8,128)(2,1)S(1)} %copy-done.1, bf16[16,2048]{1,0:T(8,128)(2,1)S(1)} %bitcast.4, bf16[128,512]{1,0:T(8,128)(2,1)S(1)} %copy-done.2, bf16[4096,128]{1,0:T(8,128)(2,1)S(1)} %copy-done, f32[128,4]{1,0:T(8,128)S(1)} %copy.12.step_size, ...), custom_call_target="tpu_custom_call" | custom-call | tf_op jit(solution)/shard_map/pallas_call | solution.py:720
  100.9 0.7 copy.16
  101.5 0.6 copy.17
Async XLA Ops:
  0.6 1.1 %copy-start.1 = (bf16[16,4096]{1,0:T(8,128)(2,1)S(1)}, bf16[16,4096]{1,0:T(8,128)(2,1)}, u32[]{:S(2)}) copy-start(bf16[16,4096]{1,0:T(8,128)(2,1)} %q_in.1) | copy-start | bytes 393220
  0.6 0.9 copy-start.8
  1.6 0.7 copy-start.3
  1.6 0.7 copy-start.4
  1.6 0.7 copy-start.5
  1.6 0.7 copy-start.6
  1.6 0.7 copy-start.7
  2.3 1.2 %copy-start = (bf16[4096,128]{1,0:T(8,128)(2,1)S(1)}, bf16[4096,128]{1,0:T(8,128)(2,1)}, u32[]{:S(2)}) copy-start(bf16[4096,128]{1,0:T(8,128)(2,1)} %wx.1) | copy-start | bytes 3145732
  3.5 0.9 copy-start.2

commit v7 on v6

--- a/solution.py
+++ b/solution.py
@@ -431,13 +431,13 @@
             r.read[h] = read
             r.mix[h] = exact(read, b_t) * r.within[h]
 
-    def project():
+    def project(distances):
         total = jnp.zeros((TOK + 16, HD), F32)
-        for j in range(NM):
-            total = total + jnp.dot(
-                r.hall[j], r.wx[j * 512 : (j + 1) * 512], preferred_element_type=F32
-            )
-        r.ext[:, :HD] = total[8:].astype(BF16).astype(F32)
+        for d in distances:
+            j = lax.rem(m + d + NM, NM)
+            weights = r.wx[pl.ds(pl.multiple_of(j * 512, 512), 512)]
+            total = total + jnp.dot(r.hall[j], weights, preferred_element_type=F32)
+        return total
 
     def hidden_over_x():
         moves = []
@@ -539,8 +539,10 @@
     receive(2)
     inputs()
     wx_move.wait()
+    projected = project((0, 1, -1, 2, -2, 3, -3))
     pass_on(4)
-    project()
+    projected = projected + project((4,))
+    r.ext[:, :HD] = projected[8:].astype(BF16).astype(F32)
     states()
     forward = scan(0)
     next(forward)

time: 102 us -> 102 us (level); the launches traced: 102 us -> 101 us
  Pallas kernels: 96.5 us -> 95.3 us
    pallas_call x1, Pallas kernels: 96.5 us -> 95.3 us  [local(): pl.pallas_call(layer, out_shape=(jax.ShapeDtypeStruct((TOK, PER * HD), BF...]
where the time goes in v7:
time: 102 us; the launch traced here: 101 us
  Pallas kernels  95.3 us (93%)
  local copies, waits for them, and re-layouts  4.97 us (5%)
    pallas_call x1, Pallas kernels, local(): pl.pallas_call(layer, out_shape=(jax.ShapeDtypeStruct((TOK, PER * HD), BF...  95.3 us
    unnamed x22, local copies, waits for them, and re-layouts  4.97 us

profile of v7, /device:TPU:1, one launch (start us, length us, event | category | flops | bytes accessed | tf_op | source)
XLA Modules:
  0.0 101.0 jit_solution(5599525573628308590)
XLA Ops:
  0.6 0.0 copy-start.1
  0.6 0.0 copy-start.8
  0.6 0.9 copy.13
  1.5 0.0 copy-done.8
  1.6 0.0 copy-start.3
  1.6 0.0 copy-start.4
  1.6 0.0 copy-start.5
  1.6 0.0 copy-start.6
  1.6 0.0 copy-start.7
  1.6 0.1 copy.12.step_size
  1.7 0.0 copy-done.1
  1.7 0.5 copy-done.3
  2.3 0.0 copy-done.4
  2.3 0.0 copy-done.5
  2.3 0.0 copy-done.6
  2.3 0.0 copy-done.7
  2.3 0.0 copy-start
  2.3 1.2 %copy-done = bf16[4096,128]{1,0:T(8,128)(2,1)S(1)} copy-done((bf16[4096,128]{1,0:T(8,128)(2,1)S(1)}, bf16[4096,128]{1,0:T(8,128)(2,1)}, u32[]{:S(2)}) %copy-start) | copy-done | bytes 1048600
  3.5 0.0 copy-start.2
  3.5 0.9 copy-done.2
  4.4 95.3 %shard_map.113 = (bf16[128,512]{1,0:T(8,128)(2,1)S(1)}, f32[64,128]{1,0:T(8,128)S(1)}) custom-call(bf16[16,4096]{1,0:T(8,128)(2,1)S(1)} %copy-done.1, bf16[16,2048]{1,0:T(8,128)(2,1)S(1)} %bitcast.4, bf16[128,512]{1,0:T(8,128)(2,1)S(1)} %copy-done.2, bf16[4096,128]{1,0:T(8,128)(2,1)S(1)} %copy-done, f32[128,4]{1,0:T(8,128)S(1)} %copy.12.step_size, ...), custom_call_target="tpu_custom_call" | custom-call | tf_op jit(solution)/shard_map/pallas_call | solution.py:722
  99.7 0.7 copy.16
  100.4 0.6 copy.17
Async XLA Ops:
  0.6 1.1 %copy-start.1 = (bf16[16,4096]{1,0:T(8,128)(2,1)S(1)}, bf16[16,4096]{1,0:T(8,128)(2,1)}, u32[]{:S(2)}) copy-start(bf16[16,4096]{1,0:T(8,128)(2,1)} %q_in.1) | copy-start | bytes 393220
  0.6 0.9 copy-start.8
  1.6 0.7 copy-start.3
  1.6 0.7 copy-start.4
  1.6 0.7 copy-start.5
  1.6 0.7 copy-start.6
  1.6 0.7 copy-start.7
  2.3 1.2 %copy-start = (bf16[4096,128]{1,0:T(8,128)(2,1)S(1)}, bf16[4096,128]{1,0:T(8,128)(2,1)}, u32[]{:S(2)}) copy-start(bf16[4096,128]{1,0:T(8,128)(2,1)} %wx.1) | copy-start | bytes 3145732
  3.5 0.9 copy-start.2
